TPU v7x, 128 devices: a whole 4x4x4 slice. The times are simulated.
128 devices in a mesh: gy: 8 (over z_hi, y), gz: 16 (over z_lo, x, core).
Axes of the slice: x: 4, y: 4, z: 4 (z_hi: 2, z_lo: 2; z = z_hi * 2 + z_lo), core: 2. Of those that a mesh axis runs over, the one named last changes fastest.
Arguments:
- eigenvectors: bfloat16 [1, 64, 64, 16, 2, 3, 128], P(None, 'gy', 'gz'), may hold values from -6 to 6
- gauge_links: float32 [1, 3, 2, 3, 3, 64, 64, 16], P(None, None, None, None, None, 'gy', 'gz'), may hold values from -3 to 3
Outputs:
- elementals: float32 [128, 1, 4, 2, 128], P(('gy', 'gz'))
All inputs are finite; a program needn't handle non-finite values.
Results may differ from a plain program's by a relative error of at most 0.0028.
Values may be sent and summed in bfloat16 or wider, within the bound.
No kernel may reach another device: no remote copies, remote signals or barrier semaphores. Data moves between devices by JAX's collectives and lax.ppermute only.
A program may use at most 64 MiB of HBM per device.

v0:
```python
import math

import jax
import jax.numpy as jnp
from jax import lax
from jax.sharding import PartitionSpec as P


def with_halo(value, sides, width):
    for axis, dim in sides:
        size, length = (lax.axis_size(axis), value.shape[dim])
        up = [(i, (i + 1) % size) for i in range(size)]
        down = [(j, i) for i, j in up]
        last = lax.slice_in_dim(value, length - width, length, axis=dim)
        first = lax.slice_in_dim(value, 0, width, axis=dim)
        before = lax.ppermute(last, axis, up)
        after = lax.ppermute(first, axis, down)
        value = jnp.concatenate([before, value, after], axis=dim)
    return value


def passed_along(block, axis, distance):
    devices = range(lax.axis_size(axis))
    route = [((i - distance) % len(devices), i) for i in devices]
    return lax.ppermute(block, axis, route)


def transport(link_dir, source, dagger):
    link_real = jnp.transpose(link_dir[0], (2, 3, 4, 0, 1))
    link_imag = jnp.transpose(link_dir[1], (2, 3, 4, 0, 1))
    if dagger:
        link_real = jnp.swapaxes(link_real, 3, 4)
        link_imag = -jnp.swapaxes(link_imag, 3, 4)
    vec_real = source[:, :, :, 0].astype(jnp.float32)
    vec_imag = source[:, :, :, 1].astype(jnp.float32)
    out_real = jnp.zeros(vec_real.shape, jnp.float32)
    out_imag = jnp.zeros(vec_real.shape, jnp.float32)
    for colour in range(3):
        coef_real = link_real[:, :, :, :, colour][..., None]
        coef_imag = link_imag[:, :, :, :, colour][..., None]
        part_real = vec_real[:, :, :, colour : colour + 1, :]
        part_imag = vec_imag[:, :, :, colour : colour + 1, :]
        out_real = out_real + coef_real * part_real - coef_imag * part_imag
        out_imag = out_imag + coef_real * part_imag + coef_imag * part_real
    return jnp.stack([out_real, out_imag], axis=3)


def rotate(source):
    count = source.shape[2]
    angles = jnp.arange(count, dtype=jnp.float32) * (2.0 * math.pi / count)
    cosine = jnp.cos(angles)[None, None, :, None, None]
    sine = -jnp.sin(angles)[None, None, :, None, None]
    vec_real = source[:, :, :, 0].astype(jnp.float32)
    vec_imag = source[:, :, :, 1].astype(jnp.float32)
    out_real = cosine * vec_real - sine * vec_imag
    out_imag = cosine * vec_imag + sine * vec_real
    return jnp.stack([out_real, out_imag], axis=3)


def derive(link_dir, ahead_source, behind_links, behind_source):
    ahead = transport(link_dir, ahead_source, False)
    behind = transport(behind_links, behind_source, True)
    return (0.5 * (ahead - behind)).astype(jnp.bfloat16)


def elemental(left_block, image):
    width = left_block.shape[-1]
    swapped = jnp.stack([image[:, :, :, 1], -image[:, :, :, 0]], axis=3)
    right_block = jnp.concatenate([image, swapped], axis=-1)
    product = lax.dot_general(
        left_block.reshape(-1, width),
        right_block.reshape(-1, 2 * width),
        (((0,), (0,)), ((), ())),
        preferred_element_type=jnp.float32,
    )
    return product.reshape(width, 2, width)


def per_device(eigenvectors, gauge_links):
    slab_y = eigenvectors.shape[1]
    slab_z = eigenvectors.shape[2]
    count_x = eigenvectors.shape[3]
    norm_factor = (6.0 * count_x * slab_y * lax.axis_size("gy") * slab_z * lax.axis_size("gz")) ** (
        -0.5
    )
    padded = with_halo(eigenvectors, (("gy", 1), ("gz", 2)), 1)
    back_links_y = passed_along(gauge_links[:, 1, :, :, :, -1:], "gy", 1)
    back_links_z = passed_along(gauge_links[:, 2, :, :, :, :, -1:], "gz", 1)
    source = eigenvectors[0]
    links_now = gauge_links[0]
    images = [rotate(source).astype(jnp.bfloat16)]
    images.append(
        derive(
            links_now[0],
            jnp.roll(source, -1, 2),
            jnp.roll(links_now[0], 1, axis=5),
            jnp.roll(source, 1, 2),
        )
    )
    sheet = padded[0]
    lower_y = jnp.concatenate([back_links_y[0], links_now[1][:, :, :, :-1]], axis=3)
    lower_z = jnp.concatenate([back_links_z[0], links_now[2][:, :, :, :, :-1]], axis=4)
    images.append(derive(links_now[1], sheet[2:, 1:-1], lower_y, sheet[:-2, 1:-1]))
    images.append(derive(links_now[2], sheet[1:-1, 2:], lower_z, sheet[1:-1, :-2]))
    stacked = jnp.stack([elemental(source, image) for image in images], axis=1)
    partials = [stacked * norm_factor]
    partial_all = jnp.stack(partials, axis=1)
    return lax.psum_scatter(partial_all, ("gy", "gz"), scatter_dimension=0, tiled=True)


def solution(mesh):
    placed = (
        P(None, "gy", "gz", None, None, None, None),
        P(None, None, None, None, None, "gy", "gz", None),
    )
    return jax.shard_map(
        per_device,
        mesh=mesh,
        in_specs=placed,
        out_specs=P(("gy", "gz"), None, None, None, None),
        check_vma=False,
    )
```

profile of v0, /device:TPU:1, one launch (start us, length us, event | category | flops | bytes accessed | tf_op | source)
XLA Modules:
  0.0 286.4 jit_solution(4829551971361365039)
XLA Ops:
  6.5 1.2 fusion.66
  8.4 2.1 collective-permute-start
  11.1 4.8 %collective-permute-start.1 = (bf16[1,1,4,16,2,3,128]{6,3,5,4,2,1,0:T(8,128)(2,1)}, bf16[1,1,4,16,2,3,128]{6,3,5,4,2,1,0:T(8,128)(2,1)}, u32[]{:S(2)}, u32[]{:S(2)}) collective-permute-start(bf16[1,1,4,16,2,3,128]{6,3,5,4,2,1,0:T(8,128)(2,1)} %copy.149), channel_id=1, source_target_pairs={{16,0},{32,16},{48,32},{64,48},{80,64},{96,80},{112,96},{0,112},{1... | collective-permute-start | bytes 294920 | tf_op jit(solution)/shard_map/ppermute | solution.py:17
  15.9 1.4 slice_bitcast_fusion.89
  17.3 1.7 slice.507
  18.9 2.1 collective-permute-start.5
  25.6 1.0 copy.104
  26.6 1.0 copy.105
  27.5 1.0 copy.106
  28.5 1.0 copy.107
  29.5 1.0 copy.108
  30.5 1.0 copy.109
  32.2 1.0 copy.103
  33.2 1.0 copy.98
  34.1 1.0 copy.99
  35.1 1.4 reshape_squeeze.2
  36.5 1.1 copy.110
  37.7 1.7 copy.114
  39.4 1.8 copy.115
  41.2 1.0 copy.116
  42.2 1.0 copy.117
  43.1 1.0 copy.118
  44.1 1.0 copy.126
  45.1 1.0 copy.127
  46.1 1.0 copy.128
  47.0 1.0 copy.129
  48.0 1.0 copy.130
  48.9 1.0 copy.131
  50.8 1.0 copy.120
  51.7 1.0 copy.121
  52.7 1.0 copy.122
  53.6 1.0 copy.123
  54.6 1.0 copy.124
  55.6 1.0 copy.125
  56.5 1.0 fusion.43
  57.5 1.0 copy.133
  58.5 1.0 copy.134
  59.5 1.0 copy.135
  60.5 1.0 copy.136
  61.4 1.0 copy.137
  62.4 1.0 copy.138
  64.7 0.9 copy-done.2
  68.3 3.8 %multiply_subtract_fusion.4 = (f32[8,4,16,1,3,128]{5,4,3,2,1,0:T(4,128)S(1)}, f32[8,4,16,1,3,128]{5,4,3,2,1,0:T(4,128)S(1)}) fusion(f32[8,4,16,128]{3,2,1,0:T(8,128)S(1)} %get-tuple-element.54, f32[8,4,16,3]{3,2,1,0:T(8,128)S(1)} %copy-done.37, f32[8,4,16,128]{3,2,1,0:T(8,128)S(1)} %get-tuple-element.51, f32[8,4,16,3]{3,2,1,0:T(8,128)S(1)} %copy-done.36, ...), kind=kLoop, calls=%fused_computation.39 | loop fusion | flops 4325376 | bytes 3182592 | tf_op jit(solution)/shard_map/sub | solution.py:43
  72.2 3.9 %multiply_subtract_fusion.5 = (f32[8,4,16,1,3,128]{5,4,3,2,1,0:T(4,128)S(1)}, f32[8,4,16,1,3,128]{5,4,3,2,1,0:T(4,128)S(1)}) fusion(f32[8,4,16,128]{3,2,1,0:T(8,128)S(1)} %get-tuple-element.64, f32[8,4,16,3]{3,2,1,0:T(8,128)S(1)} %copy-done.29, f32[8,4,16,128]{3,2,1,0:T(8,128)S(1)} %get-tuple-element.61, f32[8,4,16,3]{3,2,1,0:T(8,128)S(1)} %copy.102, ...), kind=kLoop, calls=%fused_computation.41 | loop fusion | flops 4325376 | bytes 3182592 | tf_op jit(solution)/shard_map/sub | solution.py:43
  77.4 1.4 convert_element_type.123
  80.7 0.9 copy-done.38
  81.9 1.3 fusion.10
  87.3 1.6 concatenate.55
  89.0 1.4 convert_element_type.113
  90.3 2.0 fusion.6
  93.1 1.2 maximum_bitcast_fusion
  94.3 1.5 fusion.35
  97.3 3.9 %multiply_subtract_fusion.2 = (f32[8,4,16,1,3,128]{5,4,3,2,1,0:T(4,128)S(1)}, f32[8,4,16,1,3,128]{5,4,3,2,1,0:T(4,128)S(1)}) fusion(f32[8,4,16,128]{3,2,1,0:T(8,128)S(1)} %get-tuple-element.72, f32[8,4,16,3]{3,2,1,0:T(8,128)S(1)} %copy-done.28, f32[8,4,16,128]{3,2,1,0:T(8,128)S(1)} %get-tuple-element.143, f32[8,4,16,3]{3,2,1,0:T(8,128)S(1)} %copy-done.27, ...), kind=kLoop, calls=%fused_computation.35 | loop fusion | flops 4325376 | bytes 3182592 | tf_op jit(solution)/shard_map/sub | solution.py:43
  101.2 3.9 %multiply_subtract_fusion.3 = (f32[8,4,16,1,3,128]{5,4,3,2,1,0:T(4,128)S(1)}, f32[8,4,16,1,3,128]{5,4,3,2,1,0:T(4,128)S(1)}) fusion(f32[8,4,16,128]{3,2,1,0:T(8,128)S(1)} %get-tuple-element.78, f32[8,4,16,3]{3,2,1,0:T(8,128)S(1)} %copy-done.16, f32[8,4,16,128]{3,2,1,0:T(8,128)S(1)} %get-tuple-element.146, f32[8,4,16,3]{3,2,1,0:T(8,128)S(1)} %copy-done.15, ...), kind=kLoop, calls=%fused_computation.37 | loop fusion | flops 4325376 | bytes 3182592 | tf_op jit(solution)/shard_map/sub | solution.py:43
  106.0 1.3 fusion.60
  107.3 1.4 convert_element_type.133
  108.7 1.2 slice_bitcast_fusion.15
  111.3 3.9 %multiply_subtract_fusion = (f32[8,4,16,1,3,128]{5,4,3,2,1,0:T(4,128)S(1)}, f32[8,4,16,1,3,128]{5,4,3,2,1,0:T(4,128)S(1)}) fusion(f32[8,4,16,128]{3,2,1,0:T(8,128)S(1)} %get-tuple-element.84, f32[8,4,16,3]{3,2,1,0:T(8,128)S(1)} %copy-done.22, f32[8,4,16,128]{3,2,1,0:T(8,128)S(1)} %get-tuple-element.137, f32[8,4,16,3]{3,2,1,0:T(8,128)S(1)} %copy-done.21, ...), kind=kLoop, calls=%fused_computation.31 | loop fusion | flops 4325376 | bytes 3182592 | tf_op jit(solution)/shard_map/sub | solution.py:43
  115.2 3.9 %multiply_subtract_fusion.1 = (f32[8,4,16,1,3,128]{5,4,3,2,1,0:T(4,128)S(1)}, f32[8,4,16,1,3,128]{5,4,3,2,1,0:T(4,128)S(1)}) fusion(f32[8,4,16,128]{3,2,1,0:T(8,128)S(1)} %get-tuple-element.90, f32[8,4,16,3]{3,2,1,0:T(8,128)S(1)} %copy-done.11, f32[8,4,16,128]{3,2,1,0:T(8,128)S(1)} %get-tuple-element.140, f32[8,4,16,3]{3,2,1,0:T(8,128)S(1)} %copy-done.10, ...), kind=kLoop, calls=%fused_computation.33 | loop fusion | flops 4325376 | bytes 3182592 | tf_op jit(solution)/shard_map/sub | solution.py:43
  120.4 1.4 convert_element_type.143
  122.5 1.4 concatenate.65
  123.9 2.0 fusion.14
  129.5 1.3 maximum_multiply_fusion
  130.9 147.4 %all-reduce.3.cloned.1.call-done = f32[128,1,4,2,128]{4,2,3,1,0:T(4,128)} async-done(((f32[128,1,4,2,128]{4,2,3,1,0:T(4,128)}), f32[128,1,4,2,128]{4,2,3,1,0:T(4,128)}) %all-reduce.3.cloned.1.call-update) | async-done | bytes 524304
  (187 shorter events, 30.4 us)
Async XLA Ops:
  6.5 14.4 %copy-start = (f32[1,3,2,3,3,8,4,16]{7,6,5,4,3,2,1,0:T(4,128)S(1)}, f32[1,3,2,3,3,8,4,16]{7,6,5,4,3,2,1,0:T(4,128)}, u32[]{:S(2)}) copy-start(f32[1,3,2,3,3,8,4,16]{7,6,5,4,3,2,1,0:T(4,128)} %param.3) | copy-start | bytes 331780
  6.5 271.8 %all-reduce.3.cloned.1.call-start = ((), (), s32[]{:S(2)}) async-start(), calls=%async_computation | async-start | bytes 1048576
  8.4 55.0 %collective-permute-start = (bf16[1,1,4,16,2,3,128]{6,3,5,4,2,1,0:T(8,128)(2,1)}, bf16[1,1,4,16,2,3,128]{6,3,5,4,2,1,0:T(8,128)(2,1)}, u32[]{:S(2)}, u32[]{:S(2)}) collective-permute-start(bf16[1,1,4,16,2,3,128]{6,3,5,4,2,1,0:T(8,128)(2,1)} %copy.148), channel_id=1, source_target_pairs={{0,16},{16,32},{32,48},{48,64},{64,80},{80,96},{96,112},{112,0},{1... | collective-permute-start | bytes 294920 | tf_op jit(solution)/shard_map/ppermute | solution.py:16
  11.1 73.1 %collective-permute-start.1 = (bf16[1,1,4,16,2,3,128]{6,3,5,4,2,1,0:T(8,128)(2,1)}, bf16[1,1,4,16,2,3,128]{6,3,5,4,2,1,0:T(8,128)(2,1)}, u32[]{:S(2)}, u32[]{:S(2)}) collective-permute-start(bf16[1,1,4,16,2,3,128]{6,3,5,4,2,1,0:T(8,128)(2,1)} %copy.149), channel_id=1, source_target_pairs={{16,0},{32,16},{48,32},{64,48},{80,64},{96,80},{112,96},{0,112},{1... | collective-permute-start | bytes 294920 | tf_op jit(solution)/shard_map/ppermute | solution.py:17
  17.3 32.6 %collective-permute-start.4 = (f32[1,2,3,3,1,4,16]{6,5,3,2,1,4,0:T(4,128)}, f32[1,2,3,3,1,4,16]{6,5,3,2,1,4,0:T(4,128)}, u32[]{:S(2)}, u32[]{:S(2)}) collective-permute-start(f32[1,2,3,3,1,4,16]{6,5,3,2,1,4,0:T(4,128)} %slice_bitcast_fusion.89), channel_id=1, source_target_pairs={{112,0},{0,16},{16,32},{32,48},{48,64},{64,80},{80,96},{96,112},{1... | collective-permute-start | bytes 13832 | tf_op jit(solution)/shard_map/ppermute | solution.py:25
  18.9 37.6 %collective-permute-start.5 = (f32[1,2,3,3,8,1,16]{6,4,3,2,1,5,0:T(8,128)}, f32[1,2,3,3,8,1,16]{6,4,3,2,1,5,0:T(8,128)}, u32[]{:S(2)}, u32[]{:S(2)}) collective-permute-start(f32[1,2,3,3,8,1,16]{6,4,3,2,1,5,0:T(8,128)} %bitcast.122), channel_id=1, source_target_pairs={{15,0},{0,1},{1,2},{2,3},{3,4},{4,5},{5,6},{6,7},{7,8},{8,9},{9,10... | collective-permute-start | bytes 27656 | tf_op jit(solution)/shard_map/ppermute | solution.py:25
  21.4 3.7 %copy-start.1 = (bf16[1,8,4,16,2,3,128]{6,4,5,3,2,1,0:T(2,128)(2,1)S(1)}, bf16[1,8,4,16,2,3,128]{6,4,5,3,2,1,0:T(2,128)(2,1)}, u32[]{:S(2)}) copy-start(bf16[1,8,4,16,2,3,128]{6,4,5,3,2,1,0:T(2,128)(2,1)} %param.2) | copy-start | bytes 2359300
  23.7 1.9 copy-start.57
  23.7 2.9 %copy-start.56 = (f32[8,4,16,3]{2,1,0,3:T(4,128)S(1)}, f32[8,4,16,3]{2,1,0,3:T(4,128)}, u32[]{:S(2)}) copy-start(f32[8,4,16,3]{2,1,0,3:T(4,128)} %get-tuple-element.103) | copy-start | bytes 18436
  23.7 3.8 %copy-start.55 = (f32[8,4,16,3]{2,1,0,3:T(4,128)S(1)}, f32[8,4,16,3]{2,1,0,3:T(4,128)}, u32[]{:S(2)}) copy-start(f32[8,4,16,3]{2,1,0,3:T(4,128)} %get-tuple-element.165) | copy-start | bytes 18436
  24.4 4.1 %copy-start.54 = (f32[8,4,16,3]{2,1,0,3:T(4,128)S(1)}, f32[8,4,16,3]{2,1,0,3:T(4,128)}, u32[]{:S(2)}) copy-start(f32[8,4,16,3]{2,1,0,3:T(4,128)} %get-tuple-element.105) | copy-start | bytes 18436
  25.0 4.4 %copy-start.52 = (f32[8,4,16,3]{2,1,0,3:T(4,128)S(1)}, f32[8,4,16,3]{2,1,0,3:T(4,128)}, u32[]{:S(2)}) copy-start(f32[8,4,16,3]{2,1,0,3:T(4,128)} %get-tuple-element.166) | copy-start | bytes 18436
  25.0 6.4 %copy-start.53 = (f32[8,4,16,3]{2,1,0,3:T(4,128)S(1)}, f32[8,4,16,3]{2,1,0,3:T(4,128)}, u32[]{:S(2)}) copy-start(f32[8,4,16,3]{2,1,0,3:T(4,128)} %get-tuple-element.154) | copy-start | bytes 18436
  25.6 6.1 %copy-start.51 = (f32[8,4,16,3]{2,1,0,3:T(4,128)S(1)}, f32[8,4,16,3]{2,1,0,3:T(4,128)}, u32[]{:S(2)}) copy-start(f32[8,4,16,3]{2,1,0,3:T(4,128)} %get-tuple-element.111) | copy-start | bytes 18436
  36.5 4.7 %copy-start.49 = (f32[8,4,16,3]{2,1,0,3:T(4,128)S(1)}, f32[8,4,16,3]{2,1,0,3:T(4,128)}, u32[]{:S(2)}) copy-start(f32[8,4,16,3]{2,1,0,3:T(4,128)} %get-tuple-element.123) | copy-start | bytes 18436
  36.5 5.7 %copy-start.47 = (f32[8,4,16,3]{2,1,0,3:T(4,128)S(1)}, f32[8,4,16,3]{2,1,0,3:T(4,128)}, u32[]{:S(2)}) copy-start(f32[8,4,16,3]{2,1,0,3:T(4,128)} %get-tuple-element.152) | copy-start | bytes 18436
  36.5 6.7 %copy-start.45 = (f32[8,4,16,3]{2,1,0,3:T(4,128)S(1)}, f32[8,4,16,3]{2,1,0,3:T(4,128)}, u32[]{:S(2)}) copy-start(f32[8,4,16,3]{2,1,0,3:T(4,128)} %get-tuple-element.122) | copy-start | bytes 18436
  36.5 7.6 %copy-start.50 = (f32[8,4,16,3]{2,1,0,3:T(4,128)S(1)}, f32[8,4,16,3]{2,1,0,3:T(4,128)}, u32[]{:S(2)}) copy-start(f32[8,4,16,3]{2,1,0,3:T(4,128)} %get-tuple-element.150) | copy-start | bytes 18436
  36.5 8.6 %copy-start.48 = (f32[8,4,16,3]{2,1,0,3:T(4,128)S(1)}, f32[8,4,16,3]{2,1,0,3:T(4,128)}, u32[]{:S(2)}) copy-start(f32[8,4,16,3]{2,1,0,3:T(4,128)} %get-tuple-element.133) | copy-start | bytes 18436
  36.5 9.6 %copy-start.46 = (f32[8,4,16,3]{2,1,0,3:T(4,128)S(1)}, f32[8,4,16,3]{2,1,0,3:T(4,128)}, u32[]{:S(2)}) copy-start(f32[8,4,16,3]{2,1,0,3:T(4,128)} %get-tuple-element.148) | copy-start | bytes 18436
  67.0 1.0 copy-start.30
  67.0 1.0 copy-start.32
  67.0 1.1 copy-start.33
  67.0 1.2 copy-start.35
  67.0 1.2 copy-start.36
  67.0 1.3 copy-start.37
  68.3 3.9 %copy-start.29 = (f32[8,4,16,3]{3,2,1,0:T(8,128)S(1)}, f32[8,4,16,3]{3,2,1,0:T(8,128)}, u32[]{:S(2)}) copy-start(f32[8,4,16,3]{3,2,1,0:T(8,128)} %copy.103) | copy-start | bytes 18436
  68.3 3.9 %copy-start.31 = (f32[8,4,16,3]{3,2,1,0:T(8,128)S(1)}, f32[8,4,16,3]{3,2,1,0:T(8,128)}, u32[]{:S(2)}) copy-start(f32[8,4,16,3]{3,2,1,0:T(8,128)} %copy.98) | copy-start | bytes 18436
  68.3 3.9 %copy-start.34 = (f32[8,4,16,3]{3,2,1,0:T(8,128)S(1)}, f32[8,4,16,3]{3,2,1,0:T(8,128)}, u32[]{:S(2)}) copy-start(f32[8,4,16,3]{3,2,1,0:T(8,128)} %copy.99) | copy-start | bytes 18436
  78.8 1.4 copy-start.59
  78.8 1.4 copy-start.60
  80.5 1.1 copy-start.38
  80.5 1.4 copy-start.41
  83.2 1.3 copy-start.3
  86.2 6.9 %collective-permute-start.2 = (bf16[1,10,1,16,2,3,128]{6,3,5,4,2,1,0:T(8,128)(2,1)}, bf16[1,10,1,16,2,3,128]{6,3,5,4,2,1,0:T(8,128)(2,1)}, u32[]{:S(2)}, u32[]{:S(2)}) collective-permute-start(bf16[1,10,1,16,2,3,128]{6,3,5,4,2,1,0:T(8,128)(2,1)} %get-tuple-element.31), channel_id=1, source_target_pairs={{0,1},{1,2},{2,3},{3,4},{4,5},{5,6},{6,7},{7,8},{8,9},{9,10},{10,1... | collective-permute-start | bytes 737288 | tf_op jit(solution)/shard_map/ppermute | solution.py:16
  86.2 6.9 %collective-permute-start.3 = (bf16[1,10,1,16,2,3,128]{6,3,5,4,2,1,0:T(8,128)(2,1)}, bf16[1,10,1,16,2,3,128]{6,3,5,4,2,1,0:T(8,128)(2,1)}, u32[]{:S(2)}, u32[]{:S(2)}) collective-permute-start(bf16[1,10,1,16,2,3,128]{6,3,5,4,2,1,0:T(8,128)(2,1)} %get-tuple-element.32), channel_id=1, source_target_pairs={{1,0},{2,1},{3,2},{4,3},{5,4},{6,5},{7,6},{8,7},{9,8},{10,9},{11,1... | collective-permute-start | bytes 737288 | tf_op jit(solution)/shard_map/ppermute | solution.py:17
  89.0 1.4 copy-start.39
  95.9 1.0 copy-start.23
  95.9 1.0 copy-start.24
  95.9 1.1 copy-start.25
  96.0 1.2 copy-start.26
  96.0 1.2 copy-start.27
  96.0 1.3 copy-start.28
  97.3 3.9 %copy-start.12 = (f32[8,4,16,3]{3,2,1,0:T(8,128)S(1)}, f32[8,4,16,3]{3,2,1,0:T(8,128)}, u32[]{:S(2)}) copy-start(f32[8,4,16,3]{3,2,1,0:T(8,128)} %copy.114) | copy-start | bytes 18436
  97.3 3.9 %copy-start.13 = (f32[8,4,16,3]{3,2,1,0:T(8,128)S(1)}, f32[8,4,16,3]{3,2,1,0:T(8,128)}, u32[]{:S(2)}) copy-start(f32[8,4,16,3]{3,2,1,0:T(8,128)} %copy.115) | copy-start | bytes 18436
  97.3 3.9 %copy-start.14 = (f32[8,4,16,3]{3,2,1,0:T(8,128)S(1)}, f32[8,4,16,3]{3,2,1,0:T(8,128)}, u32[]{:S(2)}) copy-start(f32[8,4,16,3]{3,2,1,0:T(8,128)} %copy.116) | copy-start | bytes 18436
  97.3 3.9 %copy-start.15 = (f32[8,4,16,3]{3,2,1,0:T(8,128)S(1)}, f32[8,4,16,3]{3,2,1,0:T(8,128)}, u32[]{:S(2)}) copy-start(f32[8,4,16,3]{3,2,1,0:T(8,128)} %copy.117) | copy-start | bytes 18436
  97.3 3.9 %copy-start.16 = (f32[8,4,16,3]{3,2,1,0:T(8,128)S(1)}, f32[8,4,16,3]{3,2,1,0:T(8,128)}, u32[]{:S(2)}) copy-start(f32[8,4,16,3]{3,2,1,0:T(8,128)} %copy.118) | copy-start | bytes 18436
  109.9 1.0 copy-start.18
  109.9 1.1 copy-start.19
  110.0 1.2 copy-start.20
  110.0 1.2 copy-start.21
  110.0 1.3 copy-start.22
  111.3 3.9 %copy-start.6 = (f32[8,4,16,3]{3,2,1,0:T(8,128)S(1)}, f32[8,4,16,3]{3,2,1,0:T(8,128)}, u32[]{:S(2)}) copy-start(f32[8,4,16,3]{3,2,1,0:T(8,128)} %copy.126) | copy-start | bytes 18436
  111.3 3.9 %copy-start.7 = (f32[8,4,16,3]{3,2,1,0:T(8,128)S(1)}, f32[8,4,16,3]{3,2,1,0:T(8,128)}, u32[]{:S(2)}) copy-start(f32[8,4,16,3]{3,2,1,0:T(8,128)} %copy.127) | copy-start | bytes 18436
  111.3 3.9 %copy-start.8 = (f32[8,4,16,3]{3,2,1,0:T(8,128)S(1)}, f32[8,4,16,3]{3,2,1,0:T(8,128)}, u32[]{:S(2)}) copy-start(f32[8,4,16,3]{3,2,1,0:T(8,128)} %copy.128) | copy-start | bytes 18436
  111.3 3.9 %copy-start.9 = (f32[8,4,16,3]{3,2,1,0:T(8,128)S(1)}, f32[8,4,16,3]{3,2,1,0:T(8,128)}, u32[]{:S(2)}) copy-start(f32[8,4,16,3]{3,2,1,0:T(8,128)} %copy.129) | copy-start | bytes 18436
  111.3 3.9 %copy-start.10 = (f32[8,4,16,3]{3,2,1,0:T(8,128)S(1)}, f32[8,4,16,3]{3,2,1,0:T(8,128)}, u32[]{:S(2)}) copy-start(f32[8,4,16,3]{3,2,1,0:T(8,128)} %copy.130) | copy-start | bytes 18436
  111.3 3.9 %copy-start.11 = (f32[8,4,16,3]{3,2,1,0:T(8,128)S(1)}, f32[8,4,16,3]{3,2,1,0:T(8,128)}, u32[]{:S(2)}) copy-start(f32[8,4,16,3]{3,2,1,0:T(8,128)} %copy.131) | copy-start | bytes 18436
  120.0 1.7 copy-start.4
  120.0 1.7 copy-start.5
  122.5 1.4 copy-start.40
  127.4 1.1 copy-start.42
  128.5 1.0 copy-start.44
  (4 other events, 3.7 us)
Sparse Core Ops, SparseCore 0:
  131.0 147.2 all-reduce.2
where the time goes:
time: 287 us; the launch traced here: 286 us
  waiting for transfers between devices  147 us (51%)
  local copies, waits for them, and re-layouts  71.5 us (25%)
  other arithmetic  38 us (13%)
  between operations  14.2 us (5%)
  starting transfers between devices  9.45 us (3%)
  matrix products  5.83 us (2%)
    unnamed x2, waiting for transfers between devices  147 us
    mul x50, local copies, waits for them, and re-layouts, transport(): out_real = out_real + coef_real * part_real - coef_imag * part_imag  39.3 us
    sub x6, other arithmetic, transport(): out_real = out_real + coef_real * part_real - coef_imag * part_imag  23.1 us
    unnamed x127, local copies, waits for them, and re-layouts  10.4 us
    dot_general x4, matrix products, elemental(): lax.dot_general(left_block.reshape(-1, width), right_block.reshape(-1, 2...  5.83 us
  transfers between devices with their start and end apart: 7, of which 1 were waited for; matrix products, arithmetic and copies ran while one was open for 24% of the time, Pallas kernels for 0%

commit v1 on v0

v1 whole, which is shorter than its diff:
```python
import functools

import jax
import jax.numpy as jnp
import ml_dtypes
import numpy as np
from jax import lax
from jax.experimental import pallas as pl
from jax.experimental.pallas import tpu as pltpu
from jax.sharding import PartitionSpec as P

BF16 = ml_dtypes.bfloat16


def split(value):
    high = value.astype(BF16)
    low = (value - high.astype(np.float32)).astype(BF16)
    return high, low


def row_at(x, colour, part):
    return (x * 3 + colour) * 2 + part


def constants(count):
    rows = 6 * count
    swap = np.zeros((rows, rows), np.float32)
    spin = np.zeros((rows, rows), np.float32)
    angles = np.arange(count, dtype=np.float32) * np.float32(2.0 * np.pi / count)
    cosine, sine = np.cos(angles), -np.sin(angles)
    for x in range(count):
        for colour in range(3):
            re, im = row_at(x, colour, 0), row_at(x, colour, 1)
            swap[re, im], swap[im, re] = -1.0, 1.0
            spin[re, re], spin[re, im] = cosine[x], -sine[x]
            spin[im, im], spin[im, re] = cosine[x], sine[x]
    fixed = np.zeros((2, rows, 2, 128), BF16)
    fixed[0, :, 0, :rows] = swap.astype(BF16)
    fixed[1, :, 0, :rows], fixed[1, :, 1, :rows] = split(spin)
    spread = np.zeros((2, 2, 128, 2, 2, 128), np.float32)
    masks = np.zeros((2, rows, 2, 128), np.float32)
    for shift in range(2):
        for x in range(count):
            there = (x + shift) % count
            for colour in range(3):
                for part in range(2):
                    for to_part in range(2):
                        lane = ((part ^ to_part) * 3 + colour) * count + x
                        sign = -1.0 if (part, to_part) == (0, 1) else 1.0
                        for half in range(2):
                            spread[shift, half, lane, part, half, row_at(there, colour, to_part)] = sign
            masks[shift, 6 * x : 6 * x + 6, :, 6 * there : 6 * there + 6] = 1.0
    return (
        fixed.reshape(2 * rows, 256),
        spread.reshape(2, 256, 512).astype(BF16),
        masks.reshape(2, rows, 256).astype(BF16),
    )


def kernel(
    slab_y, slab_z, count, scale, v_ref, face_y, face_z, links, fixed, spread, masks, out,
    coefs, left, right,
):
    rows = 6 * count
    sites = slab_y * slab_z
    width = v_ref.shape[1]

    def link(direction, part, colour, other):
        start = (((direction * 2 + part) * 3 + colour) * 3 + other) * sites
        return links[pl.ds(start, sites), :]

    for direction in range(3):
        flat = []
        for colour in range(3):
            pieces = [link(direction, part, colour, other) for part in range(2) for other in range(3)]
            pieces.append(jnp.zeros((sites, 128 - 6 * count), jnp.float32))
            flat.append(jnp.concatenate(pieces, axis=1))
        flat = jnp.concatenate(flat, axis=0)
        high = flat.astype(jnp.bfloat16)
        low = (flat - high.astype(jnp.float32)).astype(jnp.bfloat16)
        wide = jnp.dot(
            jnp.concatenate([high, low], axis=1),
            spread[1 if direction == 0 else 0],
            preferred_element_type=jnp.float32,
        )
        for colour in range(3):
            for part in range(2):
                for half in range(2):
                    lane = (part * 2 + half) * 128
                    value = wide[colour * sites : (colour + 1) * sites, lane : lane + 128]
                    for copy in range(4):
                        first = (half * 3 + direction) * sites * 24 + copy * 6 + colour * 2 + part
                        coefs[pl.ds(first, sites, stride=24), :] = value

    def matrix(direction, site):
        halves = []
        for half in range(2):
            start = pl.multiple_of(((half * 3 + direction) * sites + site) * 24, 24)
            value = coefs[pl.ds(start, 24), :]
            value = jnp.concatenate([value, value], axis=0).astype(jnp.bfloat16)
            halves.append(jnp.concatenate([value] * (rows // 48), axis=0))
        return jnp.concatenate(halves, axis=1) * masks[1 if direction == 0 else 0]

    def apply(matrices, source):
        padding = jnp.zeros((128 - rows, width), source.dtype)
        return jnp.dot(
            jnp.concatenate(matrices, axis=0),
            jnp.concatenate([source, padding, source, padding], axis=0),
            preferred_element_type=jnp.float32,
        ).astype(jnp.bfloat16)

    def at(site):
        return pl.ds(pl.multiple_of(site * rows, rows), rows)

    def step(y, _):
        for z in range(slab_z):
            site = y * slab_z + z
            source = v_ref[at(site), :]
            behind_y = jnp.maximum(y - 1, 0) * slab_z + z
            matrices = [fixed[...], matrix(0, site), matrix(1, behind_y)]
            if z > 0:
                matrices.append(matrix(2, site - 1))
            images = apply(matrices, source)
            left[at(site), :width] = source
            left[at(site), width:] = images[:rows]
            right[at(site), : 2 * width] = jnp.concatenate(
                [images[rows : 2 * rows], images[2 * rows : 3 * rows]], axis=1
            )
            right[at(behind_y), 2 * width : 3 * width] = images[3 * rows : 4 * rows]
            if z > 0:
                right[at(site - 1), 3 * width :] = images[4 * rows :]
        edge = y * slab_z + slab_z - 1
        right[at(edge), 3 * width :] = apply([matrix(2, edge)], face_z[at(y), :])
        return 0

    lax.fori_loop(0, slab_y, step, 0)
    for z in range(slab_z):
        edge = (slab_y - 1) * slab_z + z
        right[at(edge), 2 * width : 3 * width] = apply([matrix(1, edge)], face_y[at(z), :])

    total = lax.dot_general(
        left[...], right[...], (((0,), (0,)), ((), ())), preferred_element_type=jnp.float32
    )
    for operator in range(4):
        real = total[:width, operator * width : (operator + 1) * width]
        imag = total[width:, operator * width : (operator + 1) * width]
        if operator == 0:
            real, imag = real * scale, imag * scale
        else:
            real, imag = (real - real.T) * (0.5 * scale), (imag + imag.T) * (0.5 * scale)
        out[pl.ds(operator, width, stride=8), :] = real
        out[pl.ds(4 + operator, width, stride=8), :] = imag


def shifted(block, axis):
    size = lax.axis_size(axis)
    return lax.ppermute(block, axis, [((i + 1) % size, i) for i in range(size)])


def per_device(eigenvectors, gauge_links):
    _, slab_y, slab_z, count, _, _, width = eigenvectors.shape
    rows = 6 * count
    sites = slab_y * slab_z
    scale = (6.0 * count * slab_y * lax.axis_size("gy") * slab_z * lax.axis_size("gz")) ** (-0.5)
    field = jnp.transpose(eigenvectors[0], (0, 1, 2, 4, 3, 5)).reshape(slab_y, slab_z, rows, width)
    face_z = shifted(field[:, 0].reshape(slab_y * rows, width), "gz")
    face_y = shifted(field[0].reshape(slab_z * rows, width), "gy")
    fixed, spread, masks = constants(count)
    partial = pl.pallas_call(
        functools.partial(kernel, slab_y, slab_z, count, scale),
        out_shape=jax.ShapeDtypeStruct((8 * width, width), jnp.float32),
        scratch_shapes=[
            pltpu.VMEM((6 * sites * 24, 128), jnp.float32),
            pltpu.VMEM((sites * rows, 2 * width), jnp.bfloat16),
            pltpu.VMEM((sites * rows, 4 * width), jnp.bfloat16),
        ],
        compiler_params=pltpu.CompilerParams(vmem_limit_bytes=48 * 1024 * 1024),
    )(
        field.reshape(sites * rows, width),
        face_y,
        face_z,
        gauge_links.reshape(54 * sites, count),
        fixed,
        spread,
        masks,
    )
    gathered = lax.all_to_all(partial.reshape(width, 8, width), ("gy", "gz"), 0, 0, tiled=True)
    mine = jnp.sum(gathered, axis=0)
    return jnp.transpose(mine.reshape(2, 4, width), (1, 0, 2))[None, None]


def solution(mesh):
    placed = (
        P(None, "gy", "gz", None, None, None, None),
        P(None, None, None, None, None, "gy", "gz", None),
    )
    return jax.shard_map(
        per_device,
        mesh=mesh,
        in_specs=placed,
        out_specs=P(("gy", "gz"), None, None, None, None),
        check_vma=False,
    )
```

time: 287 us -> 46.5 us (0.16)
  waiting for transfers between devices: 147 us -> 1.64 us
  local copies, waits for them, and re-layouts: 71.5 us -> 6.65 us
  other arithmetic: 38 us -> 0.14 us
  blocking collectives: 0 us -> 24.9 us
  between operations: 14.2 us -> 0.02 us
  matrix products: 5.83 us -> 0 us
  Pallas kernels: 0 us -> 5.15 us
    unnamed x2 -> x0, waiting for transfers between devices: 147 us -> none
    mul x50 -> x0, local copies, waits for them, and re-layouts: 39.3 us -> none  [transport(): out_real = out_real + coef_real * part_real - coef_imag * part_imag]
    all_to_all x0 -> x1, blocking collectives: none -> 24.9 us  [per_device(): lax.all_to_all(partial.reshape(width, 8, width), ('gy', 'gz'), 0, 0, tile...]
    sub x7 -> x0, other arithmetic: 23.5 us -> none  [the longest x6 23.1 us: transport(): out_real = out_real + coef_real * part_real - coef_imag * part_imag]
    unnamed x127 -> x10, local copies, waits for them, and re-layouts: 10.4 us -> 4.09 us
    convert_element_type x5 -> x0, local copies, waits for them, and re-layouts: 6.02 us -> none  [the longest x3 4.12 us: derive(): return (0.5 * (ahead - behind)).astype(jnp.bfloat16)]
    dot_general x4 -> x0, matrix products: 5.83 us -> none  [elemental(): lax.dot_general(left_block.reshape(-1, width), right_block.reshape(-1, 2...]
    concatenate x5 -> x0, local copies, waits for them, and re-layouts: 5.16 us -> none  [the longest x4 4.26 us: elemental(): right_block = jnp.concatenate([image, swapped], axis=-1)]
  transfers between devices with their start and end apart: 7 -> 2, of which waited for: 1 -> 1; matrix products, arithmetic and copies ran while one was open for 24% -> 2% of each run, Pallas kernels for 0% -> 0%
where the time goes in v1:
time: 46.5 us; the launch traced here: 46.2 us
  blocking collectives  24.9 us (54%)
  starting transfers between devices  7.69 us (17%)
  local copies, waits for them, and re-layouts  6.65 us (14%)
  Pallas kernels  5.15 us (11%)
  waiting for transfers between devices  1.64 us (4%)
    all_to_all x1, blocking collectives, per_device(): lax.all_to_all(partial.reshape(width, 8, width), ('gy', 'gz'), 0, 0, tile...  24.9 us
    ppermute x2, starting transfers between devices, shifted(): return lax.ppermute(block, axis, [((i + 1) % size, i) for i in range(size)])  7.69 us
    pallas_call x1, Pallas kernels, per_device(): pl.pallas_call(functools.partial(kernel, slab_y, slab_z, count, scale), o...  5.15 us
    unnamed x10, local copies, waits for them, and re-layouts  4.09 us
    ppermute x2, waiting for transfers between devices, shifted(): return lax.ppermute(block, axis, [((i + 1) % size, i) for i in range(size)])  1.64 us
    slice x1, local copies, waits for them, and re-layouts, per_device(): face_z = shifted(field[:, 0].reshape(slab_y * rows, width), 'gz')  1 us
    slice x1, local copies, waits for them, and re-layouts, per_device(): face_y = shifted(field[0].reshape(slab_z * rows, width), 'gy')  0.96 us
  transfers between devices with their start and end apart: 2, of which 1 were waited for; matrix products, arithmetic and copies ran while one was open for 2% of the time, Pallas kernels for 0%

profile of v1, /device:TPU:1, one launch (start us, length us, event | category | flops | bytes accessed | tf_op | source)
XLA Modules:
  0.0 46.2 jit_solution(14719593393187967198)
XLA Ops:
  0.0 0.0 copy-start.2
  0.0 1.0 %slice.10 = bf16[8,1,96,128]{3,2,1,0:T(8,128)(2,1)S(1)} slice(bf16[8,4,96,128]{3,2,1,0:T(8,128)(2,1)} %bitcast.19), slice={[0:8], [0:1], [0:96], [0:128]} | slice | bytes 393216 | tf_op jit(solution)/shard_map/slice | solution.py:166
  1.0 1.5 %collective-permute-start.1 = (bf16[768,128]{1,0:T(8,128)(2,1)S(1)}, bf16[768,128]{1,0:T(8,128)(2,1)S(1)}, u32[]{:S(2)}, u32[]{:S(2)}) collective-permute-start(bf16[768,128]{1,0:T(8,128)(2,1)S(1)} %bitcast.23), channel_id=1, source_target_pairs={{1,0},{2,1},{3,2},{4,3},{5,4},{6,5},{7,6},{8,7},{9,8},{10,9},{11,1... | collective-permute-start | bytes 589832 | tf_op jit(solution)/shard_map/ppermute | solution.py:157
  2.5 1.0 %slice.9 = bf16[1,4,16,3,2,128]{5,4,3,2,1,0:T(2,128)(2,1)S(1)} slice(bf16[8,4,16,3,2,128]{5,4,3,2,1,0:T(2,128)(2,1)} %bitcast.20), slice={[0:1], [0:4], [0:16], [0:3], [0:2], [0:128]} | slice | bytes 196608 | tf_op jit(solution)/shard_map/slice | solution.py:167
  3.5 6.2 %collective-permute-start = (bf16[384,128]{1,0:T(8,128)(2,1)S(1)}, bf16[384,128]{1,0:T(8,128)(2,1)S(1)}, u32[]{:S(2)}, u32[]{:S(2)}) collective-permute-start(bf16[384,128]{1,0:T(8,128)(2,1)S(1)} %bitcast.24), channel_id=1, source_target_pairs={{16,0},{32,16},{48,32},{64,48},{80,64},{96,80},{112,96},{0,112},{1... | collective-permute-start | bytes 294920 | tf_op jit(solution)/shard_map/ppermute | solution.py:157
  9.7 1.6 %collective-permute-done.face_y = bf16[384,128]{1,0:T(8,128)(2,1)S(1)} collective-permute-done((bf16[384,128]{1,0:T(8,128)(2,1)S(1)}, bf16[384,128]{1,0:T(8,128)(2,1)S(1)}, u32[]{:S(2)}, u32[]{:S(2)}) %collective-permute-start) | collective-permute-done | bytes 98336 | tf_op jit(solution)/shard_map/ppermute | solution.py:157
  11.3 0.0 collective-permute-done.1.face_z
  11.3 0.0 copy-done.2
  11.3 0.0 copy-start
  11.3 1.1 %copy-done = bf16[1,8,4,16,2,3,128]{6,4,5,3,2,1,0:T(2,128)(2,1)S(1)} copy-done((bf16[1,8,4,16,2,3,128]{6,4,5,3,2,1,0:T(2,128)(2,1)S(1)}, bf16[1,8,4,16,2,3,128]{6,4,5,3,2,1,0:T(2,128)(2,1)}, u32[]{:S(2)}) %copy-start) | copy-done | bytes 786456
  12.4 0.0 copy-start.1
  12.4 1.2 %copy-done.1 = f32[1,3,2,3,3,8,4,16]{7,6,5,4,3,2,1,0:T(4,128)S(1)} copy-done((f32[1,3,2,3,3,8,4,16]{7,6,5,4,3,2,1,0:T(4,128)S(1)}, f32[1,3,2,3,3,8,4,16]{7,6,5,4,3,2,1,0:T(4,128)}, u32[]{:S(2)}) %copy-start.1) | copy-done | bytes 110616
  13.6 0.0 copy-start.3
  13.6 0.9 %copy-done.3 = bf16[2,96,256]{2,1,0:T(8,128)(2,1)S(1)} copy-done((bf16[2,96,256]{2,1,0:T(8,128)(2,1)S(1)}, bf16[2,96,256]{2,1,0:T(8,128)(2,1)}, u32[]{:S(2)}) %copy-start.3) | copy-done | bytes 98328
  14.5 0.0 copy-start.4
  14.5 0.9 %copy-done.4 = bf16[192,256]{1,0:T(8,128)(2,1)S(1)} copy-done((bf16[192,256]{1,0:T(8,128)(2,1)S(1)}, bf16[192,256]{1,0:T(8,128)(2,1)}, u32[]{:S(2)}) %copy-start.4) | copy-done | bytes 98328
  15.4 5.2 %shard_map.55 = f32[1024,128]{1,0:T(8,128)S(1)} custom-call(bf16[3072,128]{1,0:T(8,128)(2,1)S(1)} %bitcast.21, bf16[384,128]{1,0:T(8,128)(2,1)S(1)} %collective-permute-done.face_y, bf16[768,128]{1,0:T(8,128)(2,1)S(1)} %collective-permute-done.1.face_z, f32[1728,16]{1,0:T(8,128)S(1)} %bitcast.22, bf16[192,256]{1,0:T(8,128)(2,1)S(1)} %copy-done.4, ...), custom_call_target="tpu_custom_call" | custom-call | tf_op jit(solution)/shard_map/pallas_call | solution.py:169
  20.6 24.9 %all_to_all.5 = f32[128,8,128]{2,1,0:T(8,128)S(1)} all-to-all(f32[128,8,128]{2,1,0:T(8,128)S(1)} %bitcast.18), channel_id=1, replica_groups=mesh['gy'=8,'gz'=16] {'gy','gz'}, dimensions={0} | all-to-all | bytes 1048576 | tf_op jit(solution)/shard_map/all_to_all | solution.py:187
  45.5 0.1 reduce_sum.9
  45.6 0.6 %copy.8 = f32[1,1,4,2,128]{4,3,2,1,0:T(2,128)} copy(f32[1,1,4,2,128]{4,2,3,1,0:T(4,128)S(1)} %bitcast.25) | data formatting | bytes 8192 | tf_op jit(solution)/shard_map/broadcast_in_dim | solution.py:189
Async XLA Ops:
  0.0 11.3 %copy-start.2 = (bf16[2,256,512]{2,1,0:T(8,128)(2,1)S(1)}, bf16[2,256,512]{2,1,0:T(8,128)(2,1)}, u32[]{:S(2)}) copy-start(bf16[2,256,512]{2,1,0:T(8,128)(2,1)} %constant.9.clone.spread) | copy-start | bytes 1572868
  1.0 10.3 %collective-permute-start.1 = (bf16[768,128]{1,0:T(8,128)(2,1)S(1)}, bf16[768,128]{1,0:T(8,128)(2,1)S(1)}, u32[]{:S(2)}, u32[]{:S(2)}) collective-permute-start(bf16[768,128]{1,0:T(8,128)(2,1)S(1)} %bitcast.23), channel_id=1, source_target_pairs={{1,0},{2,1},{3,2},{4,3},{5,4},{6,5},{7,6},{8,7},{9,8},{10,9},{11,1... | collective-permute-start | bytes 589832 | tf_op jit(solution)/shard_map/ppermute | solution.py:157
  3.5 7.8 %collective-permute-start = (bf16[384,128]{1,0:T(8,128)(2,1)S(1)}, bf16[384,128]{1,0:T(8,128)(2,1)S(1)}, u32[]{:S(2)}, u32[]{:S(2)}) collective-permute-start(bf16[384,128]{1,0:T(8,128)(2,1)S(1)} %bitcast.24), channel_id=1, source_target_pairs={{16,0},{32,16},{48,32},{64,48},{80,64},{96,80},{112,96},{0,112},{1... | collective-permute-start | bytes 294920 | tf_op jit(solution)/shard_map/ppermute | solution.py:157
  11.3 1.1 %copy-start = (bf16[1,8,4,16,2,3,128]{6,4,5,3,2,1,0:T(2,128)(2,1)S(1)}, bf16[1,8,4,16,2,3,128]{6,4,5,3,2,1,0:T(2,128)(2,1)}, u32[]{:S(2)}) copy-start(bf16[1,8,4,16,2,3,128]{6,4,5,3,2,1,0:T(2,128)(2,1)} %param.5) | copy-start | bytes 2359300
  12.4 1.2 %copy-start.1 = (f32[1,3,2,3,3,8,4,16]{7,6,5,4,3,2,1,0:T(4,128)S(1)}, f32[1,3,2,3,3,8,4,16]{7,6,5,4,3,2,1,0:T(4,128)}, u32[]{:S(2)}) copy-start(f32[1,3,2,3,3,8,4,16]{7,6,5,4,3,2,1,0:T(4,128)} %param.6) | copy-start | bytes 331780
  13.6 0.9 %copy-start.3 = (bf16[2,96,256]{2,1,0:T(8,128)(2,1)S(1)}, bf16[2,96,256]{2,1,0:T(8,128)(2,1)}, u32[]{:S(2)}) copy-start(bf16[2,96,256]{2,1,0:T(8,128)(2,1)} %constant.10.clone.masks) | copy-start | bytes 294916
  14.5 0.9 %copy-start.4 = (bf16[192,256]{1,0:T(8,128)(2,1)S(1)}, bf16[192,256]{1,0:T(8,128)(2,1)}, u32[]{:S(2)}) copy-start(bf16[192,256]{1,0:T(8,128)(2,1)} %constant.8.clone.fixed) | copy-start | bytes 294916

commit v2 on v1

v2 whole, which is shorter than its diff:
```python
import functools

import jax
import jax.numpy as jnp
import ml_dtypes
import numpy as np
from jax import lax
from jax.experimental import pallas as pl
from jax.experimental.pallas import tpu as pltpu
from jax.sharding import PartitionSpec as P

BF16 = ml_dtypes.bfloat16


def split(value):
    high = value.astype(BF16)
    low = (value - high.astype(np.float32)).astype(BF16)
    return high, low


def row_at(x, colour, part):
    return (x * 3 + colour) * 2 + part


def constants(count):
    rows = 6 * count
    swap = np.zeros((rows, rows), np.float32)
    spin = np.zeros((rows, rows), np.float32)
    angles = np.arange(count, dtype=np.float32) * np.float32(2.0 * np.pi / count)
    cosine, sine = np.cos(angles), -np.sin(angles)
    for x in range(count):
        for colour in range(3):
            re, im = row_at(x, colour, 0), row_at(x, colour, 1)
            swap[re, im], swap[im, re] = -1.0, 1.0
            spin[re, re], spin[re, im] = cosine[x], -sine[x]
            spin[im, im], spin[im, re] = cosine[x], sine[x]
    fixed = np.zeros((2, rows, 2, 128), BF16)
    fixed[0, :, 0, :rows] = swap.astype(BF16)
    fixed[1, :, 0, :rows], fixed[1, :, 1, :rows] = split(spin)
    spread = np.zeros((2, 2, 128, 2, 2, 128), np.float32)
    masks = np.zeros((2, rows, 2, 128), np.float32)
    for shift in range(2):
        for x in range(count):
            there = (x + shift) % count
            for colour in range(3):
                for part in range(2):
                    for to_part in range(2):
                        lane = ((part ^ to_part) * 3 + colour) * count + x
                        sign = -1.0 if (part, to_part) == (0, 1) else 1.0
                        for half in range(2):
                            spread[shift, half, lane, part, half, row_at(there, colour, to_part)] = sign
            masks[shift, 6 * x : 6 * x + 6, :, 6 * there : 6 * there + 6] = 1.0
    return (
        fixed.reshape(2 * rows, 256),
        spread.reshape(2, 256, 512).astype(BF16),
        masks.reshape(2, rows, 256).astype(BF16),
    )


def site_rows(site, rows):
    return pl.ds(pl.multiple_of(site * rows, rows), rows)


def spread_links(flat, spread):
    high = flat.astype(jnp.bfloat16)
    low = (flat - high.astype(jnp.float32)).astype(jnp.bfloat16)
    return jnp.dot(
        jnp.concatenate([high, low], axis=1), spread, preferred_element_type=jnp.float32
    )


def store_coefs(coefs, base, stride, wide, sites):
    for colour in range(3):
        for part in range(2):
            for half in range(2):
                lane = (part * 2 + half) * 128
                value = wide[colour * sites : (colour + 1) * sites, lane : lane + 128]
                for copy in range(4):
                    first = base + half * stride + copy * 6 + colour * 2 + part
                    coefs[pl.ds(first, sites, stride=24), :] = value


def block_matrix(coefs, start, stride, rows, mask):
    halves = []
    for half in range(2):
        value = coefs[pl.ds(pl.multiple_of(start + half * stride, 24), 24), :]
        value = jnp.concatenate([value, value], axis=0).astype(jnp.bfloat16)
        halves.append(jnp.concatenate([value] * (rows // 48), axis=0))
    return jnp.concatenate(halves, axis=1) * mask


def apply(matrices, source):
    rows, width = source.shape
    padding = jnp.zeros((128 - rows, width), source.dtype)
    return jnp.dot(
        jnp.concatenate(matrices, axis=0),
        jnp.concatenate([source, padding, source, padding], axis=0),
        preferred_element_type=jnp.float32,
    ).astype(jnp.bfloat16)


def faces_kernel(
    slab_y, slab_z, count, v_hbm, links_hbm, spread_hbm, masks_hbm, face_y, face_z,
    links, spread, masks, last_y, last_z, coefs, sems,
):
    rows = 6 * count
    sites = slab_y * slab_z
    used = 8 + sites
    moves = [
        pltpu.make_async_copy(links_hbm.at[pl.ds(18 * sites, 36 * sites)], links, sems.at[0]),
        pltpu.make_async_copy(spread_hbm.at[0], spread, sems.at[1]),
        pltpu.make_async_copy(masks_hbm.at[0], masks, sems.at[2]),
        pltpu.make_async_copy(
            v_hbm.at[pl.ds((slab_y - 1) * slab_z * rows, slab_z * rows)], last_y, sems.at[3]
        ),
    ]
    for y in range(slab_y):
        source = v_hbm.at[pl.ds((y * slab_z + slab_z - 1) * rows, rows)]
        moves.append(pltpu.make_async_copy(source, last_z.at[pl.ds(y * rows, rows)], sems.at[4 + y]))
    for move in moves:
        move.start()
    for move in moves[:2]:
        move.wait()
    for direction, first, number, base in ((1, sites - 8, 8, 0), (2, 0, sites, 8)):
        flat = []
        for other in range(3):
            pieces = []
            for part in range(2):
                for colour in range(3):
                    start = ((((direction - 1) * 2 + part) * 3 + colour) * 3 + other) * sites
                    piece = links[pl.ds(start + first, number), :]
                    pieces.append(-piece if part else piece)
            pieces.append(jnp.zeros((number, 128 - rows), jnp.float32))
            flat.append(jnp.concatenate(pieces, axis=1))
        wide = spread_links(jnp.concatenate(flat, axis=0), spread[...])
        store_coefs(coefs, base * 24, used * 24, wide, number)
    for move in moves[2:]:
        move.wait()
    mask = masks[...]
    for z in range(slab_z):
        matrix = block_matrix(coefs, (8 - slab_z + z) * 24, used * 24, rows, mask)
        face_y[site_rows(z, rows), :] = apply([matrix], last_y[site_rows(z, rows), :])
    for y in range(slab_y):
        matrix = block_matrix(coefs, (8 + y * slab_z + slab_z - 1) * 24, used * 24, rows, mask)
        face_z[site_rows(y, rows), :] = apply([matrix], last_z[site_rows(y, rows), :])


def local_kernel(
    slab_y, slab_z, count, v_ref, links, fixed, spread, masks, total, first_y, first_z,
    coefs, left, right,
):
    rows = 6 * count
    sites = slab_y * slab_z
    width = v_ref.shape[1]

    for direction in range(3):
        flat = []
        for colour in range(3):
            pieces = []
            for part in range(2):
                for other in range(3):
                    start = (((direction * 2 + part) * 3 + colour) * 3 + other) * sites
                    pieces.append(links[pl.ds(start, sites), :])
            pieces.append(jnp.zeros((sites, 128 - rows), jnp.float32))
            flat.append(jnp.concatenate(pieces, axis=1))
        wide = spread_links(jnp.concatenate(flat, axis=0), spread[1 if direction == 0 else 0])
        store_coefs(coefs, direction * sites * 24, 3 * sites * 24, wide, sites)

    def matrix(direction, site):
        start = (direction * sites + site) * 24
        return block_matrix(coefs, start, 3 * sites * 24, rows, masks[1 if direction == 0 else 0])

    def at(site):
        return site_rows(site, rows)

    def step(y):
        for z in range(slab_z):
            site = y * slab_z + z
            source = v_ref[at(site), :]
            matrices = [fixed[...], matrix(0, site)]
            if y > 0:
                matrices.append(matrix(1, site - slab_z))
            if z > 0:
                matrices.append(matrix(2, site - 1))
            images = apply(matrices, source)
            left[at(site), :width] = source
            left[at(site), width:] = images[:rows]
            right[at(site), : 2 * width] = jnp.concatenate(
                [images[rows : 2 * rows], images[2 * rows : 3 * rows]], axis=1
            )
            if y > 0:
                right[at(site - slab_z), 2 * width : 3 * width] = images[3 * rows : 4 * rows]
            if z > 0:
                right[at(site - 1), 3 * width :] = images[-rows:]
            else:
                first_z[at(y), :] = left[at(site), :]
        right[at(y * slab_z + slab_z - 1), 3 * width :] = jnp.zeros((rows, width), jnp.bfloat16)

    for y in range(slab_y):
        step(y)
    first_y[...] = left[pl.ds(0, slab_z * rows), :]
    last = pl.ds((slab_y - 1) * slab_z * rows, slab_z * rows)
    right[last, 2 * width : 3 * width] = jnp.zeros((slab_z * rows, width), jnp.bfloat16)
    total[...] = lax.dot_general(
        left[...], right[...], (((0,), (0,)), ((), ())), preferred_element_type=jnp.float32
    )


def edge_kernel(scale, total, first_y, first_z, face_y, face_z, out, sums):
    width = face_y.shape[1]

    def product(first, face):
        return lax.dot_general(
            first[...], face[...], (((0,), (0,)), ((), ())), preferred_element_type=jnp.float32
        )

    extra = {2: product(first_y, face_y), 3: product(first_z, face_z)}
    for operator in range(4):
        both = total[:, operator * width : (operator + 1) * width]
        if operator in extra:
            both = both - extra[operator]
        real, imag = both[:width], both[width:]
        if operator == 0:
            real, imag = real * scale, imag * scale
        else:
            real, imag = (real - real.T) * (0.5 * scale), (imag + imag.T) * (0.5 * scale)
        sums[pl.ds(2 * operator, width, stride=8), :] = real
        sums[pl.ds(2 * operator + 1, width, stride=8), :] = imag
    out[...] = sums[...].astype(jnp.bfloat16)


def shifted(block, axis):
    size = lax.axis_size(axis)
    return lax.ppermute(block, axis, [(i, (i + 1) % size) for i in range(size)])


def per_device(eigenvectors, gauge_links):
    _, slab_y, slab_z, count, _, _, width = eigenvectors.shape
    rows = 6 * count
    sites = slab_y * slab_z
    scale = (6.0 * count * slab_y * lax.axis_size("gy") * slab_z * lax.axis_size("gz")) ** (-0.5)
    field = jnp.transpose(eigenvectors[0], (0, 1, 2, 4, 3, 5)).reshape(sites * rows, width)
    links = gauge_links.reshape(54 * sites, count)
    fixed, spread, masks = constants(count)
    face_y, face_z = pl.pallas_call(
        functools.partial(faces_kernel, slab_y, slab_z, count),
        out_shape=[
            jax.ShapeDtypeStruct((slab_z * rows, width), jnp.bfloat16),
            jax.ShapeDtypeStruct((slab_y * rows, width), jnp.bfloat16),
        ],
        in_specs=[pl.BlockSpec(memory_space=pltpu.HBM)] * 4,
        scratch_shapes=[
            pltpu.VMEM((36 * sites, count), jnp.float32),
            pltpu.VMEM(spread.shape[1:], jnp.bfloat16),
            pltpu.VMEM(masks.shape[1:], jnp.bfloat16),
            pltpu.VMEM((slab_z * rows, width), jnp.bfloat16),
            pltpu.VMEM((slab_y * rows, width), jnp.bfloat16),
            pltpu.VMEM((2 * (8 + sites) * 24, 128), jnp.float32),
            pltpu.SemaphoreType.DMA((4 + slab_y,)),
        ],
        compiler_params=pltpu.CompilerParams(vmem_limit_bytes=60 * 1024 * 1024),
        cost_estimate=pl.CostEstimate(flops=10_000_000_000, bytes_accessed=600_000, transcendentals=0),
    )(field, links, spread, masks)
    face_y = shifted(face_y, "gy")
    face_z = shifted(face_z, "gz")
    total, first_y, first_z = pl.pallas_call(
        functools.partial(local_kernel, slab_y, slab_z, count),
        out_shape=[
            jax.ShapeDtypeStruct((2 * width, 4 * width), jnp.float32),
            jax.ShapeDtypeStruct((slab_z * rows, 2 * width), jnp.bfloat16),
            jax.ShapeDtypeStruct((slab_y * rows, 2 * width), jnp.bfloat16),
        ],
        scratch_shapes=[
            pltpu.VMEM((6 * sites * 24, 128), jnp.float32),
            pltpu.VMEM((sites * rows, 2 * width), jnp.bfloat16),
            pltpu.VMEM((sites * rows, 4 * width), jnp.bfloat16),
        ],
        compiler_params=pltpu.CompilerParams(vmem_limit_bytes=32 * 1024 * 1024),
        cost_estimate=pl.CostEstimate(flops=5_000_000_000, bytes_accessed=4_000_000, transcendentals=0),
    )(field, links, fixed, spread, masks)
    partial = pl.pallas_call(
        functools.partial(edge_kernel, scale),
        out_shape=jax.ShapeDtypeStruct((8 * width, width), jnp.bfloat16),
        scratch_shapes=[pltpu.VMEM((8 * width, width), jnp.float32)],
        compiler_params=pltpu.CompilerParams(vmem_limit_bytes=16 * 1024 * 1024),
    )(total, first_y, first_z, face_y, face_z)
    gathered = lax.all_to_all(partial.reshape(width, 8, width), ("gy", "gz"), 0, 0, tiled=True)
    return jnp.sum(gathered.astype(jnp.float32), axis=0).reshape(1, 1, 4, 2, width)


def solution(mesh):
    placed = (
        P(None, "gy", "gz", None, None, None, None),
        P(None, None, None, None, None, "gy", "gz", None),
    )
    return jax.shard_map(
        per_device,
        mesh=mesh,
        in_specs=placed,
        out_specs=P(("gy", "gz"), None, None, None, None),
        check_vma=False,
    )
```

time: 46.5 us -> 33.6 us (0.72)
  local copies, waits for them, and re-layouts: 6.65 us -> 0.02 us
  blocking collectives: 24.9 us -> 19.8 us
  starting transfers between devices: 7.69 us -> 4.25 us
  Pallas kernels: 5.15 us -> 6.64 us
  other arithmetic: 0.14 us -> 0.73 us
    all_to_all x1, blocking collectives: 24.9 us -> 19.8 us  [per_device(): lax.all_to_all(partial.reshape(width, 8, width), ('gy', 'gz'), 0, 0, tile...]
    unnamed x10, local copies, waits for them, and re-layouts: 4.09 us -> 0.02 us
    ppermute x2, starting transfers between devices: 7.69 us -> 4.25 us  [shifted(): return lax.ppermute(block, axis, [(i, (i + 1) % size) for i in range(size)])]
    slice x2 -> x0, local copies, waits for them, and re-layouts: 1.96 us -> none  [the longest x1 1 us: per_device(): face_z = shifted(field[:, 0].reshape(slab_y * rows, width), 'gz')]
    pallas_call x1 -> x3, Pallas kernels: 5.15 us -> 6.64 us  [the longest x1 3.41 us: per_device(): pl.pallas_call(functools.partial(local_kernel, slab_y, slab_z, count), ou...]
    broadcast_in_dim x1 -> x0, local copies, waits for them, and re-layouts: 0.6 us -> none  [per_device(): return jnp.transpose(mine.reshape(2, 4, width), (1, 0, 2))[None, None]]
    reduce_sum x1, other arithmetic: 0.14 us -> 0.73 us  [per_device(): jnp.sum(gathered.astype(jnp.float32), axis=0).reshape(1, 1, 4, 2, width)]
  transfers between devices with their start and end apart: 2 -> 2, of which waited for: 1 -> 1; matrix products, arithmetic and copies ran while one was open for 2% -> 0% of each run, Pallas kernels for 0% -> 10%
where the time goes in v2:
time: 33.6 us; the launch traced here: 33.5 us
  blocking collectives  19.8 us (59%)
  Pallas kernels  6.64 us (20%)
  starting transfers between devices  4.25 us (13%)
  waiting for transfers between devices  1.99 us (6%)
  other arithmetic  0.73 us (2%)
    all_to_all x1, blocking collectives, per_device(): lax.all_to_all(partial.reshape(width, 8, width), ('gy', 'gz'), 0, 0, tile...  19.8 us
    ppermute x2, starting transfers between devices, shifted(): return lax.ppermute(block, axis, [(i, (i + 1) % size) for i in range(size)])  4.25 us
    pallas_call x1, Pallas kernels, per_device(): pl.pallas_call(functools.partial(local_kernel, slab_y, slab_z, count), ou...  3.41 us
    pallas_call x1, Pallas kernels, per_device(): pl.pallas_call(functools.partial(faces_kernel, slab_y, slab_z, count), ou...  2.79 us
    ppermute x2, waiting for transfers between devices, shifted(): return lax.ppermute(block, axis, [(i, (i + 1) % size) for i in range(size)])  1.99 us
    reduce_sum x1, other arithmetic, per_device(): jnp.sum(gathered.astype(jnp.float32), axis=0).reshape(1, 1, 4, 2, width)  0.73 us
  transfers between devices with their start and end apart: 2, of which 1 were waited for; matrix products, arithmetic and copies ran while one was open for 0% of the time, Pallas kernels for 10%

profile of v2, /device:TPU:1, one launch (start us, length us, event | category | flops | bytes accessed | tf_op | source)
XLA Modules:
  0.0 33.5 jit_solution(2961134631897402423)
XLA Ops:
  0.0 0.0 copy-start
  0.0 0.0 copy-start.1
  0.0 0.0 copy-start.2
  0.0 0.0 copy-start.3
  0.0 0.0 copy-start.4
  0.0 2.8 %shard_map.56 = (bf16[384,128]{1,0:T(8,128)(2,1)}, bf16[768,128]{1,0:T(8,128)(2,1)}) custom-call(bf16[3072,128]{1,0:T(8,128)(2,1)} %bitcast.11, f32[1728,16]{1,0:T(8,128)} %bitcast.9, bf16[2,256,512]{2,1,0:T(8,128)(2,1)} %constant.8.clone.spread.spread_hbm, bf16[2,96,256]{2,1,0:T(8,128)(2,1)} %constant.9.clone.masks.masks_hbm), custom_call_target="tpu_custom_call" | custom-call | flops 10000000000 | bytes 600000 | tf_op jit(solution)/shard_map/pallas_call | solution.py:245
  2.8 2.2 %collective-permute-start = (bf16[384,128]{1,0:T(8,128)(2,1)}, bf16[384,128]{1,0:T(8,128)(2,1)S(1)}, u32[]{:S(2)}, u32[]{:S(2)}) collective-permute-start(bf16[384,128]{1,0:T(8,128)(2,1)} %get-tuple-element.13), channel_id=1, source_target_pairs={{0,16},{16,32},{32,48},{48,64},{64,80},{80,96},{96,112},{112,0},{1... | collective-permute-start | bytes 294920 | tf_op jit(solution)/shard_map/ppermute | solution.py:234
  5.0 2.1 %collective-permute-start.1 = (bf16[768,128]{1,0:T(8,128)(2,1)}, bf16[768,128]{1,0:T(8,128)(2,1)S(1)}, u32[]{:S(2)}, u32[]{:S(2)}) collective-permute-start(bf16[768,128]{1,0:T(8,128)(2,1)} %get-tuple-element.14), channel_id=1, source_target_pairs={{0,1},{1,2},{2,3},{3,4},{4,5},{5,6},{6,7},{7,8},{8,9},{9,10},{10,1... | collective-permute-start | bytes 589832 | tf_op jit(solution)/shard_map/ppermute | solution.py:234
  7.1 0.0 copy-done
  7.1 0.0 copy-done.1
  7.1 0.0 copy-done.2
  7.1 0.0 copy-done.3
  7.1 0.0 copy-done.4
  7.1 3.4 %shard_map.55 = (f32[256,512]{1,0:T(8,128)S(1)}, bf16[384,256]{1,0:T(8,128)(2,1)S(1)}, bf16[768,256]{1,0:T(8,128)(2,1)S(1)}) custom-call(bf16[3072,128]{1,0:T(8,128)(2,1)S(1)} %bitcast.12, f32[1728,16]{1,0:T(8,128)S(1)} %bitcast.10, bf16[192,256]{1,0:T(8,128)(2,1)S(1)} %copy-done.4, bf16[2,256,512]{2,1,0:T(8,128)(2,1)S(1)} %copy-done.2, ...), custom_call_target="tpu_custom_call" | custom-call | flops 5000000000 | bytes 4000000 | tf_op jit(solution)/shard_map/pallas_call | solution.py:266
  10.5 2.0 %collective-permute-done.face_y = bf16[384,128]{1,0:T(8,128)(2,1)S(1)} collective-permute-done((bf16[384,128]{1,0:T(8,128)(2,1)}, bf16[384,128]{1,0:T(8,128)(2,1)S(1)}, u32[]{:S(2)}, u32[]{:S(2)}) %collective-permute-start) | collective-permute-done | bytes 98336 | tf_op jit(solution)/shard_map/ppermute | solution.py:234
  12.5 0.0 collective-permute-done.1.face_z
  12.5 0.4 %shard_map.57 = bf16[1024,128]{1,0:T(8,128)(2,1)S(1)} custom-call(f32[256,512]{1,0:T(8,128)S(1)} %get-tuple-element.10.total, bf16[384,256]{1,0:T(8,128)(2,1)S(1)} %get-tuple-element.11.first_y, bf16[768,256]{1,0:T(8,128)(2,1)S(1)} %get-tuple-element.12.first_z, bf16[384,128]{1,0:T(8,128)(2,1)S(1)} %collective-permute-done.face_y, ...), custom_call_target="tpu_custom_call" | custom-call | tf_op jit(solution)/shard_map/pallas_call | solution.py:281
  13.0 19.8 %all_to_all.5 = bf16[128,8,128]{2,1,0:T(8,128)(2,1)S(1)} all-to-all(bf16[128,8,128]{2,1,0:T(8,128)(2,1)S(1)} %bitcast.8), channel_id=1, replica_groups=mesh['gy'=8,'gz'=16] {'gy','gz'}, dimensions={0} | all-to-all | bytes 524288 | tf_op jit(solution)/shard_map/all_to_all | solution.py:287
  32.7 0.7 %convert_reduce_fusion = f32[8,128]{1,0:T(8,128)} fusion(bf16[128,8,128]{2,1,0:T(8,128)(2,1)S(1)} %all_to_all.5), kind=kLoop, calls=%fused_computation | loop fusion | flops 261120 | bytes 266240 | tf_op jit(solution)/shard_map/reduce_sum | solution.py:288
Async XLA Ops:
  0.0 7.1 %copy-start = (f32[1,3,2,3,3,8,4,16]{7,6,5,4,3,2,1,0:T(4,128)S(1)}, f32[1,3,2,3,3,8,4,16]{7,6,5,4,3,2,1,0:T(4,128)}, u32[]{:S(2)}) copy-start(f32[1,3,2,3,3,8,4,16]{7,6,5,4,3,2,1,0:T(4,128)} %param.6) | copy-start | bytes 331780
  0.0 7.1 %copy-start.1 = (bf16[1,8,4,16,2,3,128]{6,4,5,3,2,1,0:T(2,128)(2,1)S(1)}, bf16[1,8,4,16,2,3,128]{6,4,5,3,2,1,0:T(2,128)(2,1)}, u32[]{:S(2)}) copy-start(bf16[1,8,4,16,2,3,128]{6,4,5,3,2,1,0:T(2,128)(2,1)} %param.5) | copy-start | bytes 2359300
  0.0 7.1 %copy-start.2 = (bf16[2,256,512]{2,1,0:T(8,128)(2,1)S(1)}, bf16[2,256,512]{2,1,0:T(8,128)(2,1)}, u32[]{:S(2)}) copy-start(bf16[2,256,512]{2,1,0:T(8,128)(2,1)} %constant.8.clone.spread.spread_hbm) | copy-start | bytes 1572868
  0.0 7.1 %copy-start.3 = (bf16[2,96,256]{2,1,0:T(8,128)(2,1)S(1)}, bf16[2,96,256]{2,1,0:T(8,128)(2,1)}, u32[]{:S(2)}) copy-start(bf16[2,96,256]{2,1,0:T(8,128)(2,1)} %constant.9.clone.masks.masks_hbm) | copy-start | bytes 294916
  0.0 7.1 %copy-start.4 = (bf16[192,256]{1,0:T(8,128)(2,1)S(1)}, bf16[192,256]{1,0:T(8,128)(2,1)}, u32[]{:S(2)}) copy-start(bf16[192,256]{1,0:T(8,128)(2,1)} %constant.10.clone.fixed) | copy-start | bytes 294916
  2.8 9.7 %collective-permute-start = (bf16[384,128]{1,0:T(8,128)(2,1)}, bf16[384,128]{1,0:T(8,128)(2,1)S(1)}, u32[]{:S(2)}, u32[]{:S(2)}) collective-permute-start(bf16[384,128]{1,0:T(8,128)(2,1)} %get-tuple-element.13), channel_id=1, source_target_pairs={{0,16},{16,32},{32,48},{48,64},{64,80},{80,96},{96,112},{112,0},{1... | collective-permute-start | bytes 294920 | tf_op jit(solution)/shard_map/ppermute | solution.py:234
  5.0 7.5 %collective-permute-start.1 = (bf16[768,128]{1,0:T(8,128)(2,1)}, bf16[768,128]{1,0:T(8,128)(2,1)S(1)}, u32[]{:S(2)}, u32[]{:S(2)}) collective-permute-start(bf16[768,128]{1,0:T(8,128)(2,1)} %get-tuple-element.14), channel_id=1, source_target_pairs={{0,1},{1,2},{2,3},{3,4},{4,5},{5,6},{6,7},{7,8},{8,9},{9,10},{10,1... | collective-permute-start | bytes 589832 | tf_op jit(solution)/shard_map/ppermute | solution.py:234

commit v3 on v2

v3 whole, which is shorter than its diff:
```python
import functools

import jax
import jax.numpy as jnp
import ml_dtypes
import numpy as np
from jax import lax
from jax.experimental import pallas as pl
from jax.experimental.pallas import tpu as pltpu
from jax.sharding import PartitionSpec as P

BF16 = ml_dtypes.bfloat16


def split(value):
    high = value.astype(BF16)
    low = (value - high.astype(np.float32)).astype(BF16)
    return high, low


def row_at(x, colour, part):
    return (x * 3 + colour) * 2 + part


def constants(count):
    rows = 6 * count
    swap = np.zeros((rows, rows), np.float32)
    spin = np.zeros((rows, rows), np.float32)
    angles = np.arange(count, dtype=np.float32) * np.float32(2.0 * np.pi / count)
    cosine, sine = np.cos(angles), -np.sin(angles)
    for x in range(count):
        for colour in range(3):
            re, im = row_at(x, colour, 0), row_at(x, colour, 1)
            swap[re, im], swap[im, re] = -1.0, 1.0
            spin[re, re], spin[re, im] = cosine[x], -sine[x]
            spin[im, im], spin[im, re] = cosine[x], sine[x]
    fixed = np.zeros((2, rows, 2, 128), BF16)
    fixed[0, :, 0, :rows] = swap.astype(BF16)
    fixed[1, :, 0, :rows], fixed[1, :, 1, :rows] = split(spin)
    spread = np.zeros((2, 128, 2, 128), np.float32)
    masks = np.zeros((2, rows, 128), np.float32)
    for shift in range(2):
        for x in range(count):
            there = (x + shift) % count
            for colour in range(3):
                for part in range(2):
                    for to_part in range(2):
                        lane = ((part ^ to_part) * 3 + colour) * count + x
                        sign = -1.0 if (part, to_part) == (0, 1) else 1.0
                        spread[shift, lane, part, row_at(there, colour, to_part)] = sign
            masks[shift, 6 * x : 6 * x + 6, 6 * there : 6 * there + 6] = 1.0
    return (
        fixed.reshape(2 * rows, 256),
        spread.reshape(2, 128, 256).astype(BF16),
        masks.astype(BF16),
    )


def site_rows(site, rows):
    return pl.ds(pl.multiple_of(site * rows, rows), rows)


def spread_links(flat, spread):
    high = flat.astype(jnp.bfloat16)
    low = (flat - high.astype(jnp.float32)).astype(jnp.bfloat16)
    return [jnp.dot(half, spread, preferred_element_type=jnp.float32) for half in (high, low)]


def store_coefs(coefs, base, stride, wide, sites):
    for colour in range(3):
        for part in range(2):
            for half in range(2):
                value = wide[half][colour * sites : (colour + 1) * sites, part * 128 : part * 128 + 128]
                for copy in range(4):
                    first = base + half * stride + copy * 6 + colour * 2 + part
                    coefs[pl.ds(first, sites, stride=24), :] = value


def block_matrix(coefs, start, stride, rows, mask):
    halves = []
    for half in range(2):
        value = coefs[pl.ds(pl.multiple_of(start + half * stride, 24), 24), :]
        value = jnp.concatenate([value, value], axis=0).astype(jnp.bfloat16)
        halves.append(jnp.concatenate([value] * (rows // 48), axis=0) * mask)
    return jnp.concatenate(halves, axis=1)


def apply(matrices, source):
    rows, width = source.shape
    padding = jnp.zeros((128 - rows, width), source.dtype)
    return jnp.dot(
        jnp.concatenate(matrices, axis=0),
        jnp.concatenate([source, padding, source, padding], axis=0),
        preferred_element_type=jnp.float32,
    ).astype(jnp.bfloat16)


def make_face(links, spread, coefs, face, direction, first, number, chosen, count, mask, source):
    rows = 6 * count
    sites = links.shape[0] // 54
    flat = []
    for other in range(3):
        pieces = []
        for part in range(2):
            for colour in range(3):
                start = (((direction * 2 + part) * 3 + colour) * 3 + other) * sites
                piece = links[pl.ds(start + first, number), :]
                pieces.append(-piece if part else piece)
        pieces.append(jnp.zeros((number, 128 - rows), jnp.float32))
        flat.append(jnp.concatenate(pieces, axis=1))
    wide = spread_links(jnp.concatenate(flat, axis=0), spread[0])
    store_coefs(coefs, 0, number * 24, wide, number)
    mask, source = mask(), source()
    for i, site in enumerate(chosen):
        matrix = block_matrix(coefs, (site - first) * 24, number * 24, rows, mask)
        face[site_rows(i, rows), :] = apply([matrix], source[site_rows(site, rows), :])


def first_kernel(
    slab_y, slab_z, count, v_hbm, links_hbm, fixed_hbm, spread_hbm, masks_hbm,
    face_y, face_z, v_ref, links, fixed, spread, masks, coefs, sems,
):
    sites = slab_y * slab_z
    parts = [pl.ds(i * 18 * sites, 18 * sites) for i in range(3)]
    pairs = [
        (links_hbm.at[parts[1]], links.at[parts[1]]),
        (spread_hbm, spread),
        (masks_hbm, masks),
        (v_hbm, v_ref),
        (links_hbm.at[parts[2]], links.at[parts[2]]),
        (links_hbm.at[parts[0]], links.at[parts[0]]),
        (fixed_hbm, fixed),
    ]
    moves = [pltpu.make_async_copy(*pair, sems.at[i]) for i, pair in enumerate(pairs)]
    for move in moves:
        move.start()
    for move in moves[:2]:
        move.wait()

    def mask():
        moves[2].wait()
        return masks[0]

    def source():
        moves[3].wait()
        return v_ref

    chosen = range(sites - slab_z, sites)
    make_face(links, spread, coefs, face_y, 1, sites - 8, 8, chosen, count, mask, source)
    moves[4].wait()
    chosen = range(slab_z - 1, sites, slab_z)
    make_face(links, spread, coefs, face_z, 2, 0, sites, chosen, count, lambda: masks[0], lambda: v_ref)
    for move in moves[5:]:
        move.wait()


def local_kernel(
    slab_y, slab_z, count, v_ref, links, fixed, spread, masks, total, first_y, first_z,
    coefs, left, right,
):
    rows = 6 * count
    sites = slab_y * slab_z
    width = v_ref.shape[1]

    for direction in range(3):
        flat = []
        for colour in range(3):
            pieces = []
            for part in range(2):
                for other in range(3):
                    start = (((direction * 2 + part) * 3 + colour) * 3 + other) * sites
                    pieces.append(links[pl.ds(start, sites), :])
            pieces.append(jnp.zeros((sites, 128 - rows), jnp.float32))
            flat.append(jnp.concatenate(pieces, axis=1))
        wide = spread_links(jnp.concatenate(flat, axis=0), spread[1 if direction == 0 else 0])
        store_coefs(coefs, direction * sites * 24, 3 * sites * 24, wide, sites)

    def matrix(direction, site):
        start = (direction * sites + site) * 24
        return block_matrix(coefs, start, 3 * sites * 24, rows, masks[1 if direction == 0 else 0])

    def at(site):
        return site_rows(site, rows)

    def stack(source):
        padding = jnp.zeros((128 - rows, width), source.dtype)
        return jnp.concatenate([source, padding, source, padding], axis=0)

    def put(site, operator, image):
        high = image.astype(jnp.bfloat16)
        right[at(site), operator * width : (operator + 1) * width] = high
        right[at(site), (operator + 3) * width : (operator + 4) * width] = (image - high.astype(jnp.float32)).astype(jnp.bfloat16)

    for y in range(slab_y):
        for z in range(0, slab_z, 2):
            site = y * slab_z + z
            plans = []
            for here in (site, site + 1):
                plan = [(1, here, 0, here)]
                if y > 0:
                    plan.append((2, here - slab_z, 1, here - slab_z))
                if here > y * slab_z:
                    plan.append((3, here - 1, 2, here - 1))
                plans.append(plan)
            matrices = [[matrix(d, s) for _, _, d, s in plan] for plan in plans]
            columns = [stack(v_ref[at(site), :]), stack(v_ref[at(site + 1), :])]
            shared = jnp.dot(fixed[...], jnp.concatenate(columns, axis=1), preferred_element_type=jnp.float32)
            parts = [jnp.dot(jnp.concatenate(matrices[i], axis=0), columns[i], preferred_element_type=jnp.float32) for i in range(2)]
            for i, here in enumerate((site, site + 1)):
                left[at(here), :width] = v_ref[at(here), :]
                mine = shared[:, i * width : (i + 1) * width].astype(jnp.bfloat16)
                left[at(here), width:] = mine[:rows]
                right[at(here), :width] = mine[rows:]
                for j, (operator, target, _, _) in enumerate(plans[i]):
                    put(target, operator, parts[i][j * rows : (j + 1) * rows])
        first_z[at(y), :] = left[at(y * slab_z), :]
        right[at(y * slab_z + slab_z - 1), 3 * width : 4 * width] = jnp.zeros((rows, width), jnp.bfloat16)
        right[at(y * slab_z + slab_z - 1), 6 * width : 7 * width] = jnp.zeros((rows, width), jnp.bfloat16)
    first_y[...] = left[pl.ds(0, slab_z * rows), :]
    last = pl.ds((slab_y - 1) * slab_z * rows, slab_z * rows)
    right[last, 2 * width : 3 * width] = jnp.zeros((slab_z * rows, width), jnp.bfloat16)
    right[last, 5 * width : 6 * width] = jnp.zeros((slab_z * rows, width), jnp.bfloat16)
    both = lax.dot_general(
        left[...], right[...], (((0,), (0,)), ((), ())), preferred_element_type=jnp.float32
    )
    total[:, :width] = both[:, :width]
    total[:, width:] = both[:, width : 4 * width] + both[:, 4 * width :]


def edge_kernel(scale, face_z, face_y, total, first_y, first_z, out, sums):
    width = face_y.shape[1]

    def product(first, face):
        return lax.dot_general(
            first[...], face[...], (((0,), (0,)), ((), ())), preferred_element_type=jnp.float32
        )

    extra = {2: product(first_y, face_y), 3: product(first_z, face_z)}
    for operator in range(4):
        both = total[:, operator * width : (operator + 1) * width]
        if operator in extra:
            both = both - extra[operator]
        real, imag = both[:width], both[width:]
        if operator == 0:
            real, imag = real * scale, imag * scale
        else:
            real, imag = (real - real.T) * (0.5 * scale), (imag + imag.T) * (0.5 * scale)
        sums[pl.ds(2 * operator, width, stride=8), :] = real
        sums[pl.ds(2 * operator + 1, width, stride=8), :] = imag
    out[...] = sums[...].astype(jnp.bfloat16)


def shifted(block, axis):
    size = lax.axis_size(axis)
    return lax.ppermute(block, axis, [(i, (i + 1) % size) for i in range(size)])


def per_device(eigenvectors, gauge_links):
    _, slab_y, slab_z, count, _, _, width = eigenvectors.shape
    rows = 6 * count
    sites = slab_y * slab_z
    scale = (6.0 * count * slab_y * lax.axis_size("gy") * slab_z * lax.axis_size("gz")) ** (-0.5)
    field = jnp.transpose(eigenvectors[0], (0, 1, 2, 4, 3, 5)).reshape(sites * rows, width)
    links = gauge_links.reshape(54 * sites, count)
    fixed, spread, masks = constants(count)
    inputs = (field, links, fixed, spread, masks)
    face_y, face_z, *inputs = pl.pallas_call(
        functools.partial(first_kernel, slab_y, slab_z, count),
        out_shape=[
            pltpu.VMEM((slab_z * rows, width), jnp.bfloat16),
            pltpu.VMEM((slab_y * rows, width), jnp.bfloat16),
            *(pltpu.VMEM(each.shape, each.dtype) for each in inputs),
        ],
        in_specs=[pl.BlockSpec(memory_space=pltpu.HBM)] * 5,
        scratch_shapes=[
            pltpu.VMEM((2 * sites * 24, 128), jnp.float32),
            pltpu.SemaphoreType.DMA((7,)),
        ],
        compiler_params=pltpu.CompilerParams(vmem_limit_bytes=24 * 1024 * 1024),
        cost_estimate=pl.CostEstimate(flops=2_000_000_000, bytes_accessed=600_000, transcendentals=0),
    )(*(pltpu.with_memory_space_constraint(each, pltpu.HBM) for each in inputs))
    face_y = shifted(face_y, "gy")
    face_z = shifted(face_z, "gz")
    total, first_y, first_z = pl.pallas_call(
        functools.partial(local_kernel, slab_y, slab_z, count),
        out_shape=[
            jax.ShapeDtypeStruct((2 * width, 4 * width), jnp.float32),
            jax.ShapeDtypeStruct((slab_z * rows, 2 * width), jnp.bfloat16),
            jax.ShapeDtypeStruct((slab_y * rows, 2 * width), jnp.bfloat16),
        ],
        scratch_shapes=[
            pltpu.VMEM((6 * sites * 24, 128), jnp.float32),
            pltpu.VMEM((sites * rows, 2 * width), jnp.bfloat16),
            pltpu.VMEM((sites * rows, 7 * width), jnp.bfloat16),
        ],
        compiler_params=pltpu.CompilerParams(vmem_limit_bytes=32 * 1024 * 1024),
        cost_estimate=pl.CostEstimate(flops=5_000_000_000, bytes_accessed=4_000_000, transcendentals=0),
    )(*inputs)
    partial = pl.pallas_call(
        functools.partial(edge_kernel, scale),
        out_shape=jax.ShapeDtypeStruct((8 * width, width), jnp.bfloat16),
        scratch_shapes=[pltpu.VMEM((8 * width, width), jnp.float32)],
        compiler_params=pltpu.CompilerParams(vmem_limit_bytes=16 * 1024 * 1024),
    )(face_z, face_y, total, first_y, first_z)
    gathered = lax.all_to_all(partial.reshape(width, 8, width), ("gy", "gz"), 0, 0, tiled=True)
    return jnp.sum(gathered.astype(jnp.float32), axis=0).reshape(1, 1, 4, 2, width)


def solution(mesh):
    placed = (
        P(None, "gy", "gz", None, None, None, None),
        P(None, None, None, None, None, "gy", "gz", None),
    )
    return jax.shard_map(
        per_device,
        mesh=mesh,
        in_specs=placed,
        out_specs=P(("gy", "gz"), None, None, None, None),
        check_vma=False,
    )
```

time: 33.6 us -> 32.7 us (0.973)
  waiting for transfers between devices: 1.99 us -> 1.43 us
    pallas_call x1, Pallas kernels: 2.79 us -> 2.14 us  [per_device(): pl.pallas_call(functools.partial(first_kernel, slab_y, slab_z, count), ou...]
    ppermute x2, waiting for transfers between devices: 1.99 us -> 1.43 us  [shifted(): return lax.ppermute(block, axis, [(i, (i + 1) % size) for i in range(size)])]
    pallas_call x1, Pallas kernels: 3.41 us -> 3.79 us  [per_device(): pl.pallas_call(functools.partial(local_kernel, slab_y, slab_z, count), ou...]
  transfers between devices with their start and end apart: 2 -> 2, of which waited for: 1 -> 1; matrix products, arithmetic and copies ran while one was open for 0% -> 0% of each run, Pallas kernels for 10% -> 12%
where the time goes in v3:
time: 32.7 us; the launch traced here: 32.6 us
  blocking collectives  19.8 us (61%)
  Pallas kernels  6.37 us (19%)
  starting transfers between devices  4.25 us (13%)
  waiting for transfers between devices  1.43 us (4%)
  other arithmetic  0.73 us (2%)
    all_to_all x1, blocking collectives, per_device(): lax.all_to_all(partial.reshape(width, 8, width), ('gy', 'gz'), 0, 0, tile...  19.8 us
    ppermute x2, starting transfers between devices, shifted(): return lax.ppermute(block, axis, [(i, (i + 1) % size) for i in range(size)])  4.25 us
    pallas_call x1, Pallas kernels, per_device(): pl.pallas_call(functools.partial(local_kernel, slab_y, slab_z, count), ou...  3.79 us
    pallas_call x1, Pallas kernels, per_device(): pl.pallas_call(functools.partial(first_kernel, slab_y, slab_z, count), ou...  2.14 us
    ppermute x2, waiting for transfers between devices, shifted(): return lax.ppermute(block, axis, [(i, (i + 1) % size) for i in range(size)])  1.43 us
    reduce_sum x1, other arithmetic, per_device(): jnp.sum(gathered.astype(jnp.float32), axis=0).reshape(1, 1, 4, 2, width)  0.73 us
  transfers between devices with their start and end apart: 2, of which 1 were waited for; matrix products, arithmetic and copies ran while one was open for 0% of the time, Pallas kernels for 12%

profile of v3, /device:TPU:1, one launch (start us, length us, event | category | flops | bytes accessed | tf_op | source)
XLA Modules:
  0.0 32.6 jit_solution(733762830955622217)
XLA Ops:
  0.0 2.1 %shard_map.55 = (bf16[384,128]{1,0:T(8,128)(2,1)S(1)}, bf16[768,128]{1,0:T(8,128)(2,1)S(1)}, bf16[3072,128]{1,0:T(8,128)(2,1)S(1)}, f32[1728,16]{1,0:T(8,128)S(1...) custom-call(bf16[3072,128]{1,0:T(8,128)(2,1)} %bitcast.10, ...), custom_call_target="tpu_custom_call" | custom-call | flops 2000000000 | bytes 600000 | tf_op jit(solution)/shard_map/pallas_call | solution.py:267
  2.2 2.2 %collective-permute-start.1 = (bf16[384,128]{1,0:T(8,128)(2,1)S(1)}, bf16[384,128]{1,0:T(8,128)(2,1)S(1)}, u32[]{:S(2)}, u32[]{:S(2)}) collective-permute-start(bf16[384,128]{1,0:T(8,128)(2,1)S(1)} %get-tuple-element.16), channel_id=1, source_target_pairs={{0,16},{16,32},{32,48},{48,64},{64,80},{80,96},{96,112},{112,0},{1... | collective-permute-start | bytes 294920 | tf_op jit(solution)/shard_map/ppermute | solution.py:255
  4.3 2.1 %collective-permute-start = (bf16[768,128]{1,0:T(8,128)(2,1)S(1)}, bf16[768,128]{1,0:T(8,128)(2,1)S(1)}, u32[]{:S(2)}, u32[]{:S(2)}) collective-permute-start(bf16[768,128]{1,0:T(8,128)(2,1)S(1)} %get-tuple-element.15), channel_id=1, source_target_pairs={{0,1},{1,2},{2,3},{3,4},{4,5},{5,6},{6,7},{7,8},{8,9},{9,10},{10,1... | collective-permute-start | bytes 589832 | tf_op jit(solution)/shard_map/ppermute | solution.py:255
  6.4 3.8 %shard_map.56 = (f32[256,512]{1,0:T(8,128)S(1)}, bf16[384,256]{1,0:T(8,128)(2,1)S(1)}, bf16[768,256]{1,0:T(8,128)(2,1)S(1)}) custom-call(bf16[3072,128]{1,0:T(8,128)(2,1)S(1)} %get-tuple-element.17.v_ref, f32[1728,16]{1,0:T(8,128)S(1)} %get-tuple-element.18.links, bf16[192,256]{1,0:T(8,128)(2,1)S(1)} %get-tuple-element.19.fixed, ...), custom_call_target="tpu_custom_call" | custom-call | flops 5000000000 | bytes 4000000 | tf_op jit(solution)/shard_map/pallas_call | solution.py:284
  10.2 1.4 %collective-permute-done.1.face_y = bf16[384,128]{1,0:T(8,128)(2,1)S(1)} collective-permute-done((bf16[384,128]{1,0:T(8,128)(2,1)S(1)}, bf16[384,128]{1,0:T(8,128)(2,1)S(1)}, u32[]{:S(2)}, u32[]{:S(2)}) %collective-permute-start.1) | collective-permute-done | bytes 98336 | tf_op jit(solution)/shard_map/ppermute | solution.py:255
  11.6 0.0 collective-permute-done.face_z
  11.6 0.4 %shard_map.57 = bf16[1024,128]{1,0:T(8,128)(2,1)S(1)} custom-call(bf16[768,128]{1,0:T(8,128)(2,1)S(1)} %collective-permute-done.face_z, bf16[384,128]{1,0:T(8,128)(2,1)S(1)} %collective-permute-done.1.face_y, f32[256,512]{1,0:T(8,128)S(1)} %get-tuple-element.22.total, bf16[384,256]{1,0:T(8,128)(2,1)S(1)} %get-tuple-element.23.first_y, ...), custom_call_target="tpu_custom_call" | custom-call | tf_op jit(solution)/shard_map/pallas_call | solution.py:299
  12.1 19.8 %all_to_all.5 = bf16[128,8,128]{2,1,0:T(8,128)(2,1)S(1)} all-to-all(bf16[128,8,128]{2,1,0:T(8,128)(2,1)S(1)} %bitcast.8), channel_id=1, replica_groups=mesh['gy'=8,'gz'=16] {'gy','gz'}, dimensions={0} | all-to-all | bytes 524288 | tf_op jit(solution)/shard_map/all_to_all | solution.py:305
  31.8 0.7 %convert_reduce_fusion = f32[8,128]{1,0:T(8,128)} fusion(bf16[128,8,128]{2,1,0:T(8,128)(2,1)S(1)} %all_to_all.5), kind=kLoop, calls=%fused_computation | loop fusion | flops 261120 | bytes 266240 | tf_op jit(solution)/shard_map/reduce_sum | solution.py:306
Async XLA Ops:
  2.2 9.5 %collective-permute-start.1 = (bf16[384,128]{1,0:T(8,128)(2,1)S(1)}, bf16[384,128]{1,0:T(8,128)(2,1)S(1)}, u32[]{:S(2)}, u32[]{:S(2)}) collective-permute-start(bf16[384,128]{1,0:T(8,128)(2,1)S(1)} %get-tuple-element.16), channel_id=1, source_target_pairs={{0,16},{16,32},{32,48},{48,64},{64,80},{80,96},{96,112},{112,0},{1... | collective-permute-start | bytes 294920 | tf_op jit(solution)/shard_map/ppermute | solution.py:255
  4.3 7.3 %collective-permute-start = (bf16[768,128]{1,0:T(8,128)(2,1)S(1)}, bf16[768,128]{1,0:T(8,128)(2,1)S(1)}, u32[]{:S(2)}, u32[]{:S(2)}) collective-permute-start(bf16[768,128]{1,0:T(8,128)(2,1)S(1)} %get-tuple-element.15), channel_id=1, source_target_pairs={{0,1},{1,2},{2,3},{3,4},{4,5},{5,6},{6,7},{7,8},{8,9},{9,10},{10,1... | collective-permute-start | bytes 589832 | tf_op jit(solution)/shard_map/ppermute | solution.py:255

commit v4 on v3

--- a/solution.py
+++ b/solution.py
@@ -95,62 +95,63 @@
     ).astype(jnp.bfloat16)
 
 
-def make_face(links, spread, coefs, face, direction, first, number, chosen, count, mask, source):
-    rows = 6 * count
-    sites = links.shape[0] // 54
+def back_links(links, direction, first, number, count):
     flat = []
     for other in range(3):
         pieces = []
         for part in range(2):
             for colour in range(3):
-                start = (((direction * 2 + part) * 3 + colour) * 3 + other) * sites
-                piece = links[pl.ds(start + first, number), :]
+                piece = links[((direction * 2 + part) * 3 + colour) * 3 + other, pl.ds(first, number), :]
                 pieces.append(-piece if part else piece)
-        pieces.append(jnp.zeros((number, 128 - rows), jnp.float32))
+        pieces.append(jnp.zeros((number, 128 - 6 * count), jnp.float32))
         flat.append(jnp.concatenate(pieces, axis=1))
-    wide = spread_links(jnp.concatenate(flat, axis=0), spread[0])
-    store_coefs(coefs, 0, number * 24, wide, number)
-    mask, source = mask(), source()
-    for i, site in enumerate(chosen):
-        matrix = block_matrix(coefs, (site - first) * 24, number * 24, rows, mask)
-        face[site_rows(i, rows), :] = apply([matrix], source[site_rows(site, rows), :])
+    return jnp.concatenate(flat, axis=0)
 
 
 def first_kernel(
     slab_y, slab_z, count, v_hbm, links_hbm, fixed_hbm, spread_hbm, masks_hbm,
-    face_y, face_z, v_ref, links, fixed, spread, masks, coefs, sems,
+    face_y, face_z, v_ref, links, fixed, spread, masks, flat, coefs_y, coefs_z, sems,
 ):
     sites = slab_y * slab_z
-    parts = [pl.ds(i * 18 * sites, 18 * sites) for i in range(3)]
+    mine, others = pl.ds(0, slab_y - 1), pl.ds(0, slab_z - 1)
+    along_x, along_y, along_z = (pl.ds(18 * i, 18) for i in range(3))
+    whole = (slice(None),)
     pairs = [
-        (links_hbm.at[parts[1]], links.at[parts[1]]),
-        (spread_hbm, spread),
-        (masks_hbm, masks),
-        (v_hbm, v_ref),
-        (links_hbm.at[parts[2]], links.at[parts[2]]),
-        (links_hbm.at[parts[0]], links.at[parts[0]]),
-        (fixed_hbm, fixed),
+        (links_hbm, links, (along_z,)),
+        (spread_hbm, spread, whole),
+        (links_hbm, links, (along_y, pl.ds(sites - 8, 8))),
+        (masks_hbm, masks, whole),
+        (v_hbm, v_ref, (slab_y - 1,)),
+        (v_hbm, v_ref, (mine, slab_z - 1)),
+        (links_hbm, links, (along_x,)),
+        (links_hbm, links, (along_y, pl.ds(0, sites - 8))),
+        (v_hbm, v_ref, (mine, others)),
+        (fixed_hbm, fixed, whole),
     ]
-    moves = [pltpu.make_async_copy(*pair, sems.at[i]) for i, pair in enumerate(pairs)]
+    moves = [
+        pltpu.make_async_copy(source.at[where], target.at[where], sems.at[i])
+        for i, (source, target, where) in enumerate(pairs)
+    ]
     for move in moves:
         move.start()
-    for move in moves[:2]:
+    rows = 6 * count
+    for move in moves[:3]:
         move.wait()
-
-    def mask():
-        moves[2].wait()
-        return masks[0]
-
-    def source():
-        moves[3].wait()
-        return v_ref
-
-    chosen = range(sites - slab_z, sites)
-    make_face(links, spread, coefs, face_y, 1, sites - 8, 8, chosen, count, mask, source)
-    moves[4].wait()
-    chosen = range(slab_z - 1, sites, slab_z)
-    make_face(links, spread, coefs, face_z, 2, 0, sites, chosen, count, lambda: masks[0], lambda: v_ref)
-    for move in moves[5:]:
+    flat[...] = back_links(links, 2, 0, sites, count)
+    edge = flat[pl.ds(slab_z - 1, 3 * slab_y, stride=slab_z), :]
+    store_coefs(coefs_z, 0, slab_y * 24, spread_links(edge, spread[0]), slab_y)
+    edge = back_links(links, 1, sites - 8, 8, count)
+    store_coefs(coefs_y, 0, 8 * 24, spread_links(edge, spread[0]), 8)
+    for move in moves[3:6]:
+        move.wait()
+    mask = masks[0]
+    for z in range(slab_z):
+        matrix = block_matrix(coefs_y, (8 - slab_z + z) * 24, 8 * 24, rows, mask)
+        face_y[site_rows(z, rows), :] = apply([matrix], v_ref[slab_y - 1, z])
+    for y in range(slab_y):
+        matrix = block_matrix(coefs_z, y * 24, slab_y * 24, rows, mask)
+        face_z[site_rows(y, rows), :] = apply([matrix], v_ref[y, slab_z - 1])
+    for move in moves[6:]:
         move.wait()
 
 
@@ -160,7 +161,7 @@
 ):
     rows = 6 * count
     sites = slab_y * slab_z
-    width = v_ref.shape[1]
+    width = v_ref.shape[-1]
 
     for direction in range(3):
         flat = []
@@ -168,8 +169,7 @@
             pieces = []
             for part in range(2):
                 for other in range(3):
-                    start = (((direction * 2 + part) * 3 + colour) * 3 + other) * sites
-                    pieces.append(links[pl.ds(start, sites), :])
+                    pieces.append(links[((direction * 2 + part) * 3 + colour) * 3 + other])
             pieces.append(jnp.zeros((sites, 128 - rows), jnp.float32))
             flat.append(jnp.concatenate(pieces, axis=1))
         wide = spread_links(jnp.concatenate(flat, axis=0), spread[1 if direction == 0 else 0])
@@ -203,11 +203,11 @@
                     plan.append((3, here - 1, 2, here - 1))
                 plans.append(plan)
             matrices = [[matrix(d, s) for _, _, d, s in plan] for plan in plans]
-            columns = [stack(v_ref[at(site), :]), stack(v_ref[at(site + 1), :])]
+            columns = [stack(v_ref[y, z]), stack(v_ref[y, z + 1])]
             shared = jnp.dot(fixed[...], jnp.concatenate(columns, axis=1), preferred_element_type=jnp.float32)
             parts = [jnp.dot(jnp.concatenate(matrices[i], axis=0), columns[i], preferred_element_type=jnp.float32) for i in range(2)]
             for i, here in enumerate((site, site + 1)):
-                left[at(here), :width] = v_ref[at(here), :]
+                left[at(here), :width] = v_ref[y, z + i]
                 mine = shared[:, i * width : (i + 1) * width].astype(jnp.bfloat16)
                 left[at(here), width:] = mine[:rows]
                 right[at(here), :width] = mine[rows:]
@@ -260,8 +260,8 @@
     rows = 6 * count
     sites = slab_y * slab_z
     scale = (6.0 * count * slab_y * lax.axis_size("gy") * slab_z * lax.axis_size("gz")) ** (-0.5)
-    field = jnp.transpose(eigenvectors[0], (0, 1, 2, 4, 3, 5)).reshape(sites * rows, width)
-    links = gauge_links.reshape(54 * sites, count)
+    field = jnp.transpose(eigenvectors[0], (0, 1, 2, 4, 3, 5)).reshape(slab_y, slab_z, rows, width)
+    links = gauge_links.reshape(54, sites, count)
     fixed, spread, masks = constants(count)
     inputs = (field, links, fixed, spread, masks)
     face_y, face_z, *inputs = pl.pallas_call(
@@ -273,8 +273,10 @@
         ],
         in_specs=[pl.BlockSpec(memory_space=pltpu.HBM)] * 5,
         scratch_shapes=[
-            pltpu.VMEM((2 * sites * 24, 128), jnp.float32),
-            pltpu.SemaphoreType.DMA((7,)),
+            pltpu.VMEM((3 * sites, 128), jnp.float32),
+            pltpu.VMEM((2 * 8 * 24, 128), jnp.float32),
+            pltpu.VMEM((2 * slab_y * 24, 128), jnp.float32),
+            pltpu.SemaphoreType.DMA((10,)),
         ],
         compiler_params=pltpu.CompilerParams(vmem_limit_bytes=24 * 1024 * 1024),
         cost_estimate=pl.CostEstimate(flops=2_000_000_000, bytes_accessed=600_000, transcendentals=0),

time: 32.7 us -> 32.3 us (0.988)
  Pallas kernels: 6.37 us -> 6 us
    pallas_call x1, Pallas kernels: 2.14 us -> 1.77 us  [per_device(): pl.pallas_call(functools.partial(first_kernel, slab_y, slab_z, count), ou...]
where the time goes in v4:
time: 32.3 us; the launch traced here: 32.2 us
  blocking collectives  19.8 us (61%)
  Pallas kernels  6 us (19%)
  starting transfers between devices  4.25 us (13%)
  waiting for transfers between devices  1.43 us (4%)
  other arithmetic  0.73 us (2%)
    all_to_all x1, blocking collectives, per_device(): lax.all_to_all(partial.reshape(width, 8, width), ('gy', 'gz'), 0, 0, tile...  19.8 us
    ppermute x2, starting transfers between devices, shifted(): return lax.ppermute(block, axis, [(i, (i + 1) % size) for i in range(size)])  4.25 us
    pallas_call x1, Pallas kernels, per_device(): pl.pallas_call(functools.partial(local_kernel, slab_y, slab_z, count), ou...  3.79 us
    pallas_call x1, Pallas kernels, per_device(): pl.pallas_call(functools.partial(first_kernel, slab_y, slab_z, count), ou...  1.77 us
    ppermute x2, waiting for transfers between devices, shifted(): return lax.ppermute(block, axis, [(i, (i + 1) % size) for i in range(size)])  1.43 us
    reduce_sum x1, other arithmetic, per_device(): jnp.sum(gathered.astype(jnp.float32), axis=0).reshape(1, 1, 4, 2, width)  0.73 us
  transfers between devices with their start and end apart: 2, of which 1 were waited for; matrix products, arithmetic and copies ran while one was open for 0% of the time, Pallas kernels for 12%

profile of v4, /device:TPU:1, one launch (start us, length us, event | category | flops | bytes accessed | tf_op | source)
XLA Modules:
  0.0 32.2 jit_solution(15414220857363592073)
XLA Ops:
  0.0 1.8 %shard_map.55 = (bf16[384,128]{1,0:T(8,128)(2,1)S(1)}, bf16[768,128]{1,0:T(8,128)(2,1)S(1)}, bf16[8,4,96,128]{3,2,1,0:T(8,128)(2,1)S(1)}, f32[54,32,16]{2,1,0:T(...) custom-call(bf16[8,4,96,128]{3,2,1,0:T(8,128)(2,1)} %bitcast.10, ...), custom_call_target="tpu_custom_call" | custom-call | flops 2000000000 | bytes 600000 | tf_op jit(solution)/shard_map/pallas_call | solution.py:267
  1.8 2.2 %collective-permute-start.1 = (bf16[384,128]{1,0:T(8,128)(2,1)S(1)}, bf16[384,128]{1,0:T(8,128)(2,1)S(1)}, u32[]{:S(2)}, u32[]{:S(2)}) collective-permute-start(bf16[384,128]{1,0:T(8,128)(2,1)S(1)} %get-tuple-element.16), channel_id=1, source_target_pairs={{0,16},{16,32},{32,48},{48,64},{64,80},{80,96},{96,112},{112,0},{1... | collective-permute-start | bytes 294920 | tf_op jit(solution)/shard_map/ppermute | solution.py:255
  4.0 2.1 %collective-permute-start = (bf16[768,128]{1,0:T(8,128)(2,1)S(1)}, bf16[768,128]{1,0:T(8,128)(2,1)S(1)}, u32[]{:S(2)}, u32[]{:S(2)}) collective-permute-start(bf16[768,128]{1,0:T(8,128)(2,1)S(1)} %get-tuple-element.15), channel_id=1, source_target_pairs={{0,1},{1,2},{2,3},{3,4},{4,5},{5,6},{6,7},{7,8},{8,9},{9,10},{10,1... | collective-permute-start | bytes 589832 | tf_op jit(solution)/shard_map/ppermute | solution.py:255
  6.0 3.8 %shard_map.56 = (f32[256,512]{1,0:T(8,128)S(1)}, bf16[384,256]{1,0:T(8,128)(2,1)S(1)}, bf16[768,256]{1,0:T(8,128)(2,1)S(1)}) custom-call(bf16[8,4,96,128]{3,2,1,0:T(8,128)(2,1)S(1)} %get-tuple-element.17.v_ref, f32[54,32,16]{2,1,0:T(8,128)S(1)} %get-tuple-element.18.links, bf16[192,256]{1,0:T(8,128)(2,1)S(1)} %get-tuple-element.19.fixed, ...), custom_call_target="tpu_custom_call" | custom-call | flops 5000000000 | bytes 4000000 | tf_op jit(solution)/shard_map/pallas_call | solution.py:286
  9.8 1.4 %collective-permute-done.1.face_y = bf16[384,128]{1,0:T(8,128)(2,1)S(1)} collective-permute-done((bf16[384,128]{1,0:T(8,128)(2,1)S(1)}, bf16[384,128]{1,0:T(8,128)(2,1)S(1)}, u32[]{:S(2)}, u32[]{:S(2)}) %collective-permute-start.1) | collective-permute-done | bytes 98336 | tf_op jit(solution)/shard_map/ppermute | solution.py:255
  11.2 0.0 collective-permute-done.face_z
  11.3 0.4 %shard_map.57 = bf16[1024,128]{1,0:T(8,128)(2,1)S(1)} custom-call(bf16[768,128]{1,0:T(8,128)(2,1)S(1)} %collective-permute-done.face_z, bf16[384,128]{1,0:T(8,128)(2,1)S(1)} %collective-permute-done.1.face_y, f32[256,512]{1,0:T(8,128)S(1)} %get-tuple-element.22.total, bf16[384,256]{1,0:T(8,128)(2,1)S(1)} %get-tuple-element.23.first_y, ...), custom_call_target="tpu_custom_call" | custom-call | tf_op jit(solution)/shard_map/pallas_call | solution.py:301
  11.7 19.8 %all_to_all.5 = bf16[128,8,128]{2,1,0:T(8,128)(2,1)S(1)} all-to-all(bf16[128,8,128]{2,1,0:T(8,128)(2,1)S(1)} %bitcast.8), channel_id=1, replica_groups=mesh['gy'=8,'gz'=16] {'gy','gz'}, dimensions={0} | all-to-all | bytes 524288 | tf_op jit(solution)/shard_map/all_to_all | solution.py:307
  31.5 0.7 %convert_reduce_fusion = f32[8,128]{1,0:T(8,128)} fusion(bf16[128,8,128]{2,1,0:T(8,128)(2,1)S(1)} %all_to_all.5), kind=kLoop, calls=%fused_computation | loop fusion | flops 261120 | bytes 266240 | tf_op jit(solution)/shard_map/reduce_sum | solution.py:308
Async XLA Ops:
  1.8 9.5 %collective-permute-start.1 = (bf16[384,128]{1,0:T(8,128)(2,1)S(1)}, bf16[384,128]{1,0:T(8,128)(2,1)S(1)}, u32[]{:S(2)}, u32[]{:S(2)}) collective-permute-start(bf16[384,128]{1,0:T(8,128)(2,1)S(1)} %get-tuple-element.16), channel_id=1, source_target_pairs={{0,16},{16,32},{32,48},{48,64},{64,80},{80,96},{96,112},{112,0},{1... | collective-permute-start | bytes 294920 | tf_op jit(solution)/shard_map/ppermute | solution.py:255
  4.0 7.3 %collective-permute-start = (bf16[768,128]{1,0:T(8,128)(2,1)S(1)}, bf16[768,128]{1,0:T(8,128)(2,1)S(1)}, u32[]{:S(2)}, u32[]{:S(2)}) collective-permute-start(bf16[768,128]{1,0:T(8,128)(2,1)S(1)} %get-tuple-element.15), channel_id=1, source_target_pairs={{0,1},{1,2},{2,3},{3,4},{4,5},{5,6},{6,7},{7,8},{8,9},{9,10},{10,1... | collective-permute-start | bytes 589832 | tf_op jit(solution)/shard_map/ppermute | solution.py:255

commit v5 on v4

--- a/solution.py
+++ b/solution.py
@@ -12,33 +12,17 @@
 BF16 = ml_dtypes.bfloat16
 
 
-def split(value):
-    high = value.astype(BF16)
-    low = (value - high.astype(np.float32)).astype(BF16)
-    return high, low
-
-
 def row_at(x, colour, part):
     return (x * 3 + colour) * 2 + part
 
 
 def constants(count):
     rows = 6 * count
-    swap = np.zeros((rows, rows), np.float32)
-    spin = np.zeros((rows, rows), np.float32)
     angles = np.arange(count, dtype=np.float32) * np.float32(2.0 * np.pi / count)
-    cosine, sine = np.cos(angles), -np.sin(angles)
-    for x in range(count):
-        for colour in range(3):
-            re, im = row_at(x, colour, 0), row_at(x, colour, 1)
-            swap[re, im], swap[im, re] = -1.0, 1.0
-            spin[re, re], spin[re, im] = cosine[x], -sine[x]
-            spin[im, im], spin[im, re] = cosine[x], sine[x]
-    fixed = np.zeros((2, rows, 2, 128), BF16)
-    fixed[0, :, 0, :rows] = swap.astype(BF16)
-    fixed[1, :, 0, :rows], fixed[1, :, 1, :rows] = split(spin)
+    waves = np.repeat(np.stack([np.cos(angles), -np.sin(angles)]), 6, axis=1)
+    waves = np.broadcast_to(waves[..., None], (2, rows, 128)).astype(np.float32)
     spread = np.zeros((2, 128, 2, 128), np.float32)
-    masks = np.zeros((2, rows, 128), np.float32)
+    masks = np.zeros((3, rows, 128), np.float32)
     for shift in range(2):
         for x in range(count):
             there = (x + shift) % count
@@ -49,8 +33,10 @@
                         sign = -1.0 if (part, to_part) == (0, 1) else 1.0
                         spread[shift, lane, part, row_at(there, colour, to_part)] = sign
             masks[shift, 6 * x : 6 * x + 6, 6 * there : 6 * there + 6] = 1.0
+            if shift == 1:
+                masks[2, 6 * there : 6 * there + 6, 6 * x : 6 * x + 6] = -1.0
     return (
-        fixed.reshape(2 * rows, 256),
+        waves,
         spread.reshape(2, 128, 256).astype(BF16),
         masks.astype(BF16),
     )
@@ -109,8 +95,8 @@
 
 
 def first_kernel(
-    slab_y, slab_z, count, v_hbm, links_hbm, fixed_hbm, spread_hbm, masks_hbm,
-    face_y, face_z, v_ref, links, fixed, spread, masks, flat, coefs_y, coefs_z, sems,
+    slab_y, slab_z, count, v_hbm, links_hbm, waves_hbm, spread_hbm, masks_hbm,
+    face_y, face_z, v_ref, links, waves, spread, masks, flat, coefs_y, coefs_z, sems,
 ):
     sites = slab_y * slab_z
     mine, others = pl.ds(0, slab_y - 1), pl.ds(0, slab_z - 1)
@@ -126,7 +112,7 @@
         (links_hbm, links, (along_x,)),
         (links_hbm, links, (along_y, pl.ds(0, sites - 8))),
         (v_hbm, v_ref, (mine, others)),
-        (fixed_hbm, fixed, whole),
+        (waves_hbm, waves, whole),
     ]
     moves = [
         pltpu.make_async_copy(source.at[where], target.at[where], sems.at[i])
@@ -145,18 +131,20 @@
     for move in moves[3:6]:
         move.wait()
     mask = masks[0]
-    for z in range(slab_z):
-        matrix = block_matrix(coefs_y, (8 - slab_z + z) * 24, 8 * 24, rows, mask)
-        face_y[site_rows(z, rows), :] = apply([matrix], v_ref[slab_y - 1, z])
-    for y in range(slab_y):
-        matrix = block_matrix(coefs_z, y * 24, slab_y * 24, rows, mask)
-        face_z[site_rows(y, rows), :] = apply([matrix], v_ref[y, slab_z - 1])
+    jobs = [(face_y, z, coefs_y, 8 - slab_z + z, v_ref[slab_y - 1, z]) for z in range(slab_z)]
+    jobs += [(face_z, y, coefs_z, y, v_ref[y, slab_z - 1]) for y in range(slab_y)]
+    for pair in zip(jobs[::2], jobs[1::2]):
+        matrices = [block_matrix(table, at * 24, 8 * 24, rows, mask) for _, _, table, at, _ in pair]
+        images = apply(matrices, jnp.concatenate([job[4] for job in pair], axis=1))
+        for i, (face, at, *_) in enumerate(pair):
+            width = face.shape[1]
+            face[site_rows(at, rows), :] = images[i * rows : (i + 1) * rows, i * width : (i + 1) * width]
     for move in moves[6:]:
         move.wait()
 
 
 def local_kernel(
-    slab_y, slab_z, count, v_ref, links, fixed, spread, masks, total, first_y, first_z,
+    slab_y, slab_z, count, v_ref, links, waves, spread, masks, total, first_y, first_z,
     coefs, left, right,
 ):
     rows = 6 * count
@@ -173,11 +161,16 @@
             pieces.append(jnp.zeros((sites, 128 - rows), jnp.float32))
             flat.append(jnp.concatenate(pieces, axis=1))
         wide = spread_links(jnp.concatenate(flat, axis=0), spread[1 if direction == 0 else 0])
-        store_coefs(coefs, direction * sites * 24, 3 * sites * 24, wide, sites)
+        store_coefs(coefs, direction * sites * 24, 4 * sites * 24, wide, sites)
+    wide = spread_links(back_links(links, 0, 0, sites, count), spread[0])
+    store_coefs(coefs, 3 * sites * 24, 4 * sites * 24, wide, sites)
 
     def matrix(direction, site):
-        start = (direction * sites + site) * 24
-        return block_matrix(coefs, start, 3 * sites * 24, rows, masks[1 if direction == 0 else 0])
+        start, stride = (direction * sites + site) * 24, 4 * sites * 24
+        if direction > 0:
+            return block_matrix(coefs, start, stride, rows, masks[0])
+        ahead = block_matrix(coefs, start, stride, rows, masks[1])
+        return ahead + block_matrix(coefs, (3 * sites + site) * 24, stride, rows, masks[2])
 
     def at(site):
         return site_rows(site, rows)
@@ -186,10 +179,14 @@
         padding = jnp.zeros((128 - rows, width), source.dtype)
         return jnp.concatenate([source, padding, source, padding], axis=0)
 
+    is_real = lax.broadcasted_iota(jnp.int32, (rows // 8, 8, width), 1) % 2 == 0
+
     def put(site, operator, image):
         high = image.astype(jnp.bfloat16)
         right[at(site), operator * width : (operator + 1) * width] = high
-        right[at(site), (operator + 3) * width : (operator + 4) * width] = (image - high.astype(jnp.float32)).astype(jnp.bfloat16)
+        if operator > 1:
+            low = (image - high.astype(jnp.float32)).astype(jnp.bfloat16)
+            right[at(site), (operator + 2) * width : (operator + 3) * width] = low
 
     for y in range(slab_y):
         for z in range(0, slab_z, 2):
@@ -203,28 +200,32 @@
                     plan.append((3, here - 1, 2, here - 1))
                 plans.append(plan)
             matrices = [[matrix(d, s) for _, _, d, s in plan] for plan in plans]
-            columns = [stack(v_ref[y, z]), stack(v_ref[y, z + 1])]
-            shared = jnp.dot(fixed[...], jnp.concatenate(columns, axis=1), preferred_element_type=jnp.float32)
-            parts = [jnp.dot(jnp.concatenate(matrices[i], axis=0), columns[i], preferred_element_type=jnp.float32) for i in range(2)]
             for i, here in enumerate((site, site + 1)):
-                left[at(here), :width] = v_ref[y, z + i]
-                mine = shared[:, i * width : (i + 1) * width].astype(jnp.bfloat16)
-                left[at(here), width:] = mine[:rows]
-                right[at(here), :width] = mine[rows:]
+                source = v_ref[y, z + i]
+                part = jnp.dot(
+                    jnp.concatenate(matrices[i], axis=0), stack(source), preferred_element_type=jnp.float32
+                )
+                tiles = source.astype(jnp.float32).reshape(rows // 8, 8, width)
+                below, above = pltpu.roll(tiles, 7, 1), pltpu.roll(tiles, 1, 1)
+                swapped = jnp.where(is_real, -below, above).reshape(rows, width)
+                image = waves[0] * source.astype(jnp.float32) + waves[1] * swapped
+                left[at(here), :width] = source
+                left[at(here), width:] = swapped.astype(jnp.bfloat16)
+                right[at(here), :width] = image.astype(jnp.bfloat16)
                 for j, (operator, target, _, _) in enumerate(plans[i]):
-                    put(target, operator, parts[i][j * rows : (j + 1) * rows])
+                    put(target, operator, part[j * rows : (j + 1) * rows])
         first_z[at(y), :] = left[at(y * slab_z), :]
         right[at(y * slab_z + slab_z - 1), 3 * width : 4 * width] = jnp.zeros((rows, width), jnp.bfloat16)
-        right[at(y * slab_z + slab_z - 1), 6 * width : 7 * width] = jnp.zeros((rows, width), jnp.bfloat16)
+        right[at(y * slab_z + slab_z - 1), 5 * width : 6 * width] = jnp.zeros((rows, width), jnp.bfloat16)
     first_y[...] = left[pl.ds(0, slab_z * rows), :]
     last = pl.ds((slab_y - 1) * slab_z * rows, slab_z * rows)
     right[last, 2 * width : 3 * width] = jnp.zeros((slab_z * rows, width), jnp.bfloat16)
-    right[last, 5 * width : 6 * width] = jnp.zeros((slab_z * rows, width), jnp.bfloat16)
+    right[last, 4 * width : 5 * width] = jnp.zeros((slab_z * rows, width), jnp.bfloat16)
     both = lax.dot_general(
         left[...], right[...], (((0,), (0,)), ((), ())), preferred_element_type=jnp.float32
     )
-    total[:, :width] = both[:, :width]
-    total[:, width:] = both[:, width : 4 * width] + both[:, 4 * width :]
+    total[:, : 2 * width] = both[:, : 2 * width]
+    total[:, 2 * width :] = both[:, 2 * width : 4 * width] + both[:, 4 * width :]
 
 
 def edge_kernel(scale, face_z, face_y, total, first_y, first_z, out, sums):
@@ -241,8 +242,9 @@
         if operator in extra:
             both = both - extra[operator]
         real, imag = both[:width], both[width:]
-        if operator == 0:
-            real, imag = real * scale, imag * scale
+        if operator < 2:
+            factor = scale if operator == 0 else 0.5 * scale
+            real, imag = real * factor, imag * factor
         else:
             real, imag = (real - real.T) * (0.5 * scale), (imag + imag.T) * (0.5 * scale)
         sums[pl.ds(2 * operator, width, stride=8), :] = real
@@ -262,8 +264,8 @@
     scale = (6.0 * count * slab_y * lax.axis_size("gy") * slab_z * lax.axis_size("gz")) ** (-0.5)
     field = jnp.transpose(eigenvectors[0], (0, 1, 2, 4, 3, 5)).reshape(slab_y, slab_z, rows, width)
     links = gauge_links.reshape(54, sites, count)
-    fixed, spread, masks = constants(count)
-    inputs = (field, links, fixed, spread, masks)
+    waves, spread, masks = constants(count)
+    inputs = (field, links, waves, spread, masks)
     face_y, face_z, *inputs = pl.pallas_call(
         functools.partial(first_kernel, slab_y, slab_z, count),
         out_shape=[
@@ -291,9 +293,9 @@
             jax.ShapeDtypeStruct((slab_y * rows, 2 * width), jnp.bfloat16),
         ],
         scratch_shapes=[
-            pltpu.VMEM((6 * sites * 24, 128), jnp.float32),
+            pltpu.VMEM((8 * sites * 24, 128), jnp.float32),
             pltpu.VMEM((sites * rows, 2 * width), jnp.bfloat16),
-            pltpu.VMEM((sites * rows, 7 * width), jnp.bfloat16),
+            pltpu.VMEM((sites * rows, 6 * width), jnp.bfloat16),
         ],
         compiler_params=pltpu.CompilerParams(vmem_limit_bytes=32 * 1024 * 1024),
         cost_estimate=pl.CostEstimate(flops=5_000_000_000, bytes_accessed=4_000_000, transcendentals=0),

time: 32.3 us -> 32.3 us (level)
  no operation moved by 1% of the time
where the time goes in v5:
time: 32.3 us; the launch traced here: 32.2 us
  blocking collectives  19.8 us (61%)
  Pallas kernels  5.94 us (18%)
  starting transfers between devices  4.25 us (13%)
  waiting for transfers between devices  1.47 us (5%)
  other arithmetic  0.73 us (2%)
    all_to_all x1, blocking collectives, per_device(): lax.all_to_all(partial.reshape(width, 8, width), ('gy', 'gz'), 0, 0, tile...  19.8 us
    ppermute x2, starting transfers between devices, shifted(): return lax.ppermute(block, axis, [(i, (i + 1) % size) for i in range(size)])  4.25 us
    pallas_call x1, Pallas kernels, per_device(): pl.pallas_call(functools.partial(local_kernel, slab_y, slab_z, count), ou...  3.75 us
    pallas_call x1, Pallas kernels, per_device(): pl.pallas_call(functools.partial(first_kernel, slab_y, slab_z, count), ou...  1.72 us
    ppermute x2, waiting for transfers between devices, shifted(): return lax.ppermute(block, axis, [(i, (i + 1) % size) for i in range(size)])  1.47 us
    reduce_sum x1, other arithmetic, per_device(): jnp.sum(gathered.astype(jnp.float32), axis=0).reshape(1, 1, 4, 2, width)  0.73 us
  transfers between devices with their start and end apart: 2, of which 1 were waited for; matrix products, arithmetic and copies ran while one was open for 0% of the time, Pallas kernels for 12%

profile of v5, /device:TPU:1, one launch (start us, length us, event | category | flops | bytes accessed | tf_op | source)
XLA Modules:
  0.0 32.2 jit_solution(17349511739866561503)
XLA Ops:
  0.0 1.7 %shard_map.55 = (bf16[384,128]{1,0:T(8,128)(2,1)S(1)}, bf16[768,128]{1,0:T(8,128)(2,1)S(1)}, bf16[8,4,96,128]{3,2,1,0:T(8,128)(2,1)S(1)}, f32[54,32,16]{2,1,0:T(...) custom-call(bf16[8,4,96,128]{3,2,1,0:T(8,128)(2,1)} %bitcast.10, ...), custom_call_target="tpu_custom_call" | custom-call | flops 2000000000 | bytes 600000 | tf_op jit(solution)/shard_map/pallas_call | solution.py:269
  1.7 2.2 %collective-permute-start.1 = (bf16[384,128]{1,0:T(8,128)(2,1)S(1)}, bf16[384,128]{1,0:T(8,128)(2,1)S(1)}, u32[]{:S(2)}, u32[]{:S(2)}) collective-permute-start(bf16[384,128]{1,0:T(8,128)(2,1)S(1)} %get-tuple-element.16), channel_id=1, source_target_pairs={{0,16},{16,32},{32,48},{48,64},{64,80},{80,96},{96,112},{112,0},{1... | collective-permute-start | bytes 294920 | tf_op jit(solution)/shard_map/ppermute | solution.py:257
  3.9 2.0 %collective-permute-start = (bf16[768,128]{1,0:T(8,128)(2,1)S(1)}, bf16[768,128]{1,0:T(8,128)(2,1)S(1)}, u32[]{:S(2)}, u32[]{:S(2)}) collective-permute-start(bf16[768,128]{1,0:T(8,128)(2,1)S(1)} %get-tuple-element.15), channel_id=1, source_target_pairs={{0,1},{1,2},{2,3},{3,4},{4,5},{5,6},{6,7},{7,8},{8,9},{9,10},{10,1... | collective-permute-start | bytes 589832 | tf_op jit(solution)/shard_map/ppermute | solution.py:257
  6.0 3.7 %shard_map.56 = (f32[256,512]{1,0:T(8,128)S(1)}, bf16[384,256]{1,0:T(8,128)(2,1)S(1)}, bf16[768,256]{1,0:T(8,128)(2,1)S(1)}) custom-call(bf16[8,4,96,128]{3,2,1,0:T(8,128)(2,1)S(1)} %get-tuple-element.17.v_ref, f32[54,32,16]{2,1,0:T(8,128)S(1)} %get-tuple-element.18.links, f32[2,96,128]{2,1,0:T(8,128)S(1)} %get-tuple-element.19.waves, ...), custom_call_target="tpu_custom_call" | custom-call | flops 5000000000 | bytes 4000000 | tf_op jit(solution)/shard_map/pallas_call | solution.py:288
  9.7 1.5 %collective-permute-done.1.face_y = bf16[384,128]{1,0:T(8,128)(2,1)S(1)} collective-permute-done((bf16[384,128]{1,0:T(8,128)(2,1)S(1)}, bf16[384,128]{1,0:T(8,128)(2,1)S(1)}, u32[]{:S(2)}, u32[]{:S(2)}) %collective-permute-start.1) | collective-permute-done | bytes 98336 | tf_op jit(solution)/shard_map/ppermute | solution.py:257
  11.2 0.0 collective-permute-done.face_z
  11.2 0.5 %shard_map.57 = bf16[1024,128]{1,0:T(8,128)(2,1)S(1)} custom-call(bf16[768,128]{1,0:T(8,128)(2,1)S(1)} %collective-permute-done.face_z, bf16[384,128]{1,0:T(8,128)(2,1)S(1)} %collective-permute-done.1.face_y, f32[256,512]{1,0:T(8,128)S(1)} %get-tuple-element.22.total, bf16[384,256]{1,0:T(8,128)(2,1)S(1)} %get-tuple-element.23.first_y, ...), custom_call_target="tpu_custom_call" | custom-call | tf_op jit(solution)/shard_map/pallas_call | solution.py:303
  11.7 19.8 %all_to_all.5 = bf16[128,8,128]{2,1,0:T(8,128)(2,1)S(1)} all-to-all(bf16[128,8,128]{2,1,0:T(8,128)(2,1)S(1)} %bitcast.8), channel_id=1, replica_groups=mesh['gy'=8,'gz'=16] {'gy','gz'}, dimensions={0} | all-to-all | bytes 524288 | tf_op jit(solution)/shard_map/all_to_all | solution.py:309
  31.4 0.7 %convert_reduce_fusion = f32[8,128]{1,0:T(8,128)} fusion(bf16[128,8,128]{2,1,0:T(8,128)(2,1)S(1)} %all_to_all.5), kind=kLoop, calls=%fused_computation | loop fusion | flops 261120 | bytes 266240 | tf_op jit(solution)/shard_map/reduce_sum | solution.py:310
Async XLA Ops:
  1.7 9.5 %collective-permute-start.1 = (bf16[384,128]{1,0:T(8,128)(2,1)S(1)}, bf16[384,128]{1,0:T(8,128)(2,1)S(1)}, u32[]{:S(2)}, u32[]{:S(2)}) collective-permute-start(bf16[384,128]{1,0:T(8,128)(2,1)S(1)} %get-tuple-element.16), channel_id=1, source_target_pairs={{0,16},{16,32},{32,48},{48,64},{64,80},{80,96},{96,112},{112,0},{1... | collective-permute-start | bytes 294920 | tf_op jit(solution)/shard_map/ppermute | solution.py:257
  3.9 7.3 %collective-permute-start = (bf16[768,128]{1,0:T(8,128)(2,1)S(1)}, bf16[768,128]{1,0:T(8,128)(2,1)S(1)}, u32[]{:S(2)}, u32[]{:S(2)}) collective-permute-start(bf16[768,128]{1,0:T(8,128)(2,1)S(1)} %get-tuple-element.15), channel_id=1, source_target_pairs={{0,1},{1,2},{2,3},{3,4},{4,5},{5,6},{6,7},{7,8},{8,9},{9,10},{10,1... | collective-permute-start | bytes 589832 | tf_op jit(solution)/shard_map/ppermute | solution.py:257

commit v6 on v5

--- a/solution.py
+++ b/solution.py
@@ -250,6 +250,15 @@
         sums[pl.ds(2 * operator, width, stride=8), :] = real
         sums[pl.ds(2 * operator + 1, width, stride=8), :] = imag
     out[...] = sums[...].astype(jnp.bfloat16)
+
+
+def sum_kernel(gathered, out):
+    pairs = gathered.shape[0] // 16
+    sums = [jnp.zeros((16, gathered.shape[1]), jnp.float32) for _ in range(4)]
+    for i in range(pairs):
+        sums[i % 4] = sums[i % 4] + gathered[pl.ds(16 * i, 16), :].astype(jnp.float32)
+    both = (sums[0] + sums[1]) + (sums[2] + sums[3])
+    out[...] = both[:8] + both[8:]
 
 
 def shifted(block, axis):
@@ -307,7 +316,12 @@
         compiler_params=pltpu.CompilerParams(vmem_limit_bytes=16 * 1024 * 1024),
     )(face_z, face_y, total, first_y, first_z)
     gathered = lax.all_to_all(partial.reshape(width, 8, width), ("gy", "gz"), 0, 0, tiled=True)
-    return jnp.sum(gathered.astype(jnp.float32), axis=0).reshape(1, 1, 4, 2, width)
+    mine = pl.pallas_call(
+        sum_kernel,
+        out_shape=jax.ShapeDtypeStruct((8, width), jnp.float32),
+        compiler_params=pltpu.CompilerParams(vmem_limit_bytes=8 * 1024 * 1024),
+    )(gathered.reshape(8 * width, width))
+    return mine.reshape(1, 1, 4, 2, width)
 
 
 def solution(mesh):

time: 32.3 us -> 32.2 us (level)
  other arithmetic: 0.73 us -> 0 us
  Pallas kernels: 5.94 us -> 6.57 us
    reduce_sum x1 -> x0, other arithmetic: 0.73 us -> none  [per_device(): jnp.sum(gathered.astype(jnp.float32), axis=0).reshape(1, 1, 4, 2, width)]
    pallas_call x0 -> x1, Pallas kernels: none -> 0.63 us  [per_device(): pl.pallas_call(sum_kernel, out_shape=jax.ShapeDtypeStruct((8, width), jnp...]
where the time goes in v6:
time: 32.2 us; the launch traced here: 32.1 us
  blocking collectives  19.8 us (61%)
  Pallas kernels  6.57 us (20%)
  starting transfers between devices  4.25 us (13%)
  waiting for transfers between devices  1.47 us (5%)
    all_to_all x1, blocking collectives, per_device(): lax.all_to_all(partial.reshape(width, 8, width), ('gy', 'gz'), 0, 0, tile...  19.8 us
    ppermute x2, starting transfers between devices, shifted(): return lax.ppermute(block, axis, [(i, (i + 1) % size) for i in range(size)])  4.25 us
    pallas_call x1, Pallas kernels, per_device(): pl.pallas_call(functools.partial(local_kernel, slab_y, slab_z, count), ou...  3.75 us
    pallas_call x1, Pallas kernels, per_device(): pl.pallas_call(functools.partial(first_kernel, slab_y, slab_z, count), ou...  1.72 us
    ppermute x2, waiting for transfers between devices, shifted(): return lax.ppermute(block, axis, [(i, (i + 1) % size) for i in range(size)])  1.47 us
  transfers between devices with their start and end apart: 2, of which 1 were waited for; matrix products, arithmetic and copies ran while one was open for 0% of the time, Pallas kernels for 12%

profile of v6, /device:TPU:1, one launch (start us, length us, event | category | flops | bytes accessed | tf_op | source)
XLA Modules:
  0.0 32.1 jit_solution(1521757987892881637)
XLA Ops:
  0.0 1.7 %shard_map.55 = (bf16[384,128]{1,0:T(8,128)(2,1)S(1)}, bf16[768,128]{1,0:T(8,128)(2,1)S(1)}, bf16[8,4,96,128]{3,2,1,0:T(8,128)(2,1)S(1)}, f32[54,32,16]{2,1,0:T(...) custom-call(bf16[8,4,96,128]{3,2,1,0:T(8,128)(2,1)} %bitcast.12, ...), custom_call_target="tpu_custom_call" | custom-call | flops 2000000000 | bytes 600000 | tf_op jit(solution)/shard_map/pallas_call | solution.py:278
  1.7 2.2 %collective-permute-start.1 = (bf16[384,128]{1,0:T(8,128)(2,1)S(1)}, bf16[384,128]{1,0:T(8,128)(2,1)S(1)}, u32[]{:S(2)}, u32[]{:S(2)}) collective-permute-start(bf16[384,128]{1,0:T(8,128)(2,1)S(1)} %get-tuple-element.16), channel_id=1, source_target_pairs={{0,16},{16,32},{32,48},{48,64},{64,80},{80,96},{96,112},{112,0},{1... | collective-permute-start | bytes 294920 | tf_op jit(solution)/shard_map/ppermute | solution.py:266
  3.9 2.0 %collective-permute-start = (bf16[768,128]{1,0:T(8,128)(2,1)S(1)}, bf16[768,128]{1,0:T(8,128)(2,1)S(1)}, u32[]{:S(2)}, u32[]{:S(2)}) collective-permute-start(bf16[768,128]{1,0:T(8,128)(2,1)S(1)} %get-tuple-element.15), channel_id=1, source_target_pairs={{0,1},{1,2},{2,3},{3,4},{4,5},{5,6},{6,7},{7,8},{8,9},{9,10},{10,1... | collective-permute-start | bytes 589832 | tf_op jit(solution)/shard_map/ppermute | solution.py:266
  6.0 3.7 %shard_map.56 = (f32[256,512]{1,0:T(8,128)S(1)}, bf16[384,256]{1,0:T(8,128)(2,1)S(1)}, bf16[768,256]{1,0:T(8,128)(2,1)S(1)}) custom-call(bf16[8,4,96,128]{3,2,1,0:T(8,128)(2,1)S(1)} %get-tuple-element.17.v_ref, f32[54,32,16]{2,1,0:T(8,128)S(1)} %get-tuple-element.18.links, f32[2,96,128]{2,1,0:T(8,128)S(1)} %get-tuple-element.19.waves, ...), custom_call_target="tpu_custom_call" | custom-call | flops 5000000000 | bytes 4000000 | tf_op jit(solution)/shard_map/pallas_call | solution.py:297
  9.7 1.5 %collective-permute-done.1.face_y = bf16[384,128]{1,0:T(8,128)(2,1)S(1)} collective-permute-done((bf16[384,128]{1,0:T(8,128)(2,1)S(1)}, bf16[384,128]{1,0:T(8,128)(2,1)S(1)}, u32[]{:S(2)}, u32[]{:S(2)}) %collective-permute-start.1) | collective-permute-done | bytes 98336 | tf_op jit(solution)/shard_map/ppermute | solution.py:266
  11.2 0.0 collective-permute-done.face_z
  11.2 0.5 %shard_map.57 = bf16[1024,128]{1,0:T(8,128)(2,1)S(1)} custom-call(bf16[768,128]{1,0:T(8,128)(2,1)S(1)} %collective-permute-done.face_z, bf16[384,128]{1,0:T(8,128)(2,1)S(1)} %collective-permute-done.1.face_y, f32[256,512]{1,0:T(8,128)S(1)} %get-tuple-element.22.total, bf16[384,256]{1,0:T(8,128)(2,1)S(1)} %get-tuple-element.23.first_y, ...), custom_call_target="tpu_custom_call" | custom-call | tf_op jit(solution)/shard_map/pallas_call | solution.py:312
  11.7 19.8 %all_to_all.5 = bf16[128,8,128]{2,1,0:T(8,128)(2,1)S(1)} all-to-all(bf16[128,8,128]{2,1,0:T(8,128)(2,1)S(1)} %bitcast.9), channel_id=1, replica_groups=mesh['gy'=8,'gz'=16] {'gy','gz'}, dimensions={0} | all-to-all | bytes 524288 | tf_op jit(solution)/shard_map/all_to_all | solution.py:318
  31.4 0.6 %shard_map.58 = f32[8,128]{1,0:T(8,128)} custom-call(bf16[1024,128]{1,0:T(8,128)(2,1)S(1)} %bitcast.10), custom_call_target="tpu_custom_call" | custom-call | tf_op jit(solution)/shard_map/pallas_call | solution.py:319
Async XLA Ops:
  1.7 9.5 %collective-permute-start.1 = (bf16[384,128]{1,0:T(8,128)(2,1)S(1)}, bf16[384,128]{1,0:T(8,128)(2,1)S(1)}, u32[]{:S(2)}, u32[]{:S(2)}) collective-permute-start(bf16[384,128]{1,0:T(8,128)(2,1)S(1)} %get-tuple-element.16), channel_id=1, source_target_pairs={{0,16},{16,32},{32,48},{48,64},{64,80},{80,96},{96,112},{112,0},{1... | collective-permute-start | bytes 294920 | tf_op jit(solution)/shard_map/ppermute | solution.py:266
  3.9 7.3 %collective-permute-start = (bf16[768,128]{1,0:T(8,128)(2,1)S(1)}, bf16[768,128]{1,0:T(8,128)(2,1)S(1)}, u32[]{:S(2)}, u32[]{:S(2)}) collective-permute-start(bf16[768,128]{1,0:T(8,128)(2,1)S(1)} %get-tuple-element.15), channel_id=1, source_target_pairs={{0,1},{1,2},{2,3},{3,4},{4,5},{5,6},{6,7},{7,8},{8,9},{9,10},{10,1... | collective-permute-start | bytes 589832 | tf_op jit(solution)/shard_map/ppermute | solution.py:266

commit v7 on v6

--- a/solution.py
+++ b/solution.py
@@ -144,8 +144,7 @@
 
 
 def local_kernel(
-    slab_y, slab_z, count, v_ref, links, waves, spread, masks, total, first_y, first_z,
-    coefs, left, right,
+    slab_y, slab_z, count, v_ref, links, waves, spread, masks, total, turned, coefs, right
 ):
     rows = 6 * count
     sites = slab_y * slab_z
@@ -165,12 +164,14 @@
     wide = spread_links(back_links(links, 0, 0, sites, count), spread[0])
     store_coefs(coefs, 3 * sites * 24, 4 * sites * 24, wide, sites)
 
+    mask = [masks[i] for i in range(3)]
+
     def matrix(direction, site):
         start, stride = (direction * sites + site) * 24, 4 * sites * 24
         if direction > 0:
-            return block_matrix(coefs, start, stride, rows, masks[0])
-        ahead = block_matrix(coefs, start, stride, rows, masks[1])
-        return ahead + block_matrix(coefs, (3 * sites + site) * 24, stride, rows, masks[2])
+            return block_matrix(coefs, start, stride, rows, mask[0])
+        ahead = block_matrix(coefs, start, stride, rows, mask[1])
+        return ahead + block_matrix(coefs, (3 * sites + site) * 24, stride, rows, mask[2])
 
     def at(site):
         return site_rows(site, rows)
@@ -209,34 +210,38 @@
                 below, above = pltpu.roll(tiles, 7, 1), pltpu.roll(tiles, 1, 1)
                 swapped = jnp.where(is_real, -below, above).reshape(rows, width)
                 image = waves[0] * source.astype(jnp.float32) + waves[1] * swapped
-                left[at(here), :width] = source
-                left[at(here), width:] = swapped.astype(jnp.bfloat16)
+                turned[y, z + i] = swapped.astype(jnp.bfloat16)
                 right[at(here), :width] = image.astype(jnp.bfloat16)
                 for j, (operator, target, _, _) in enumerate(plans[i]):
                     put(target, operator, part[j * rows : (j + 1) * rows])
-        first_z[at(y), :] = left[at(y * slab_z), :]
         right[at(y * slab_z + slab_z - 1), 3 * width : 4 * width] = jnp.zeros((rows, width), jnp.bfloat16)
         right[at(y * slab_z + slab_z - 1), 5 * width : 6 * width] = jnp.zeros((rows, width), jnp.bfloat16)
-    first_y[...] = left[pl.ds(0, slab_z * rows), :]
     last = pl.ds((slab_y - 1) * slab_z * rows, slab_z * rows)
     right[last, 2 * width : 3 * width] = jnp.zeros((slab_z * rows, width), jnp.bfloat16)
     right[last, 4 * width : 5 * width] = jnp.zeros((slab_z * rows, width), jnp.bfloat16)
+    left = jnp.concatenate(
+        [v_ref[...].reshape(sites * rows, width), turned[...].reshape(sites * rows, width)], axis=1
+    )
     both = lax.dot_general(
-        left[...], right[...], (((0,), (0,)), ((), ())), preferred_element_type=jnp.float32
+        left, right[...], (((0,), (0,)), ((), ())), preferred_element_type=jnp.float32
     )
     total[:, : 2 * width] = both[:, : 2 * width]
     total[:, 2 * width :] = both[:, 2 * width : 4 * width] + both[:, 4 * width :]
 
 
-def edge_kernel(scale, face_z, face_y, total, first_y, first_z, out, sums):
+def edge_kernel(scale, face_z, face_y, total, v_ref, turned, out, sums):
     width = face_y.shape[1]
 
-    def product(first, face):
+    def product(parts, face):
+        first = jnp.concatenate([part.reshape(face.shape) for part in parts], axis=1)
         return lax.dot_general(
-            first[...], face[...], (((0,), (0,)), ((), ())), preferred_element_type=jnp.float32
+            first, face[...], (((0,), (0,)), ((), ())), preferred_element_type=jnp.float32
         )
 
-    extra = {2: product(first_y, face_y), 3: product(first_z, face_z)}
+    extra = {
+        2: product((v_ref[0], turned[0]), face_y),
+        3: product((v_ref[:, 0], turned[:, 0]), face_z),
+    }
     for operator in range(4):
         both = total[:, operator * width : (operator + 1) * width]
         if operator in extra:
@@ -294,16 +299,14 @@
     )(*(pltpu.with_memory_space_constraint(each, pltpu.HBM) for each in inputs))
     face_y = shifted(face_y, "gy")
     face_z = shifted(face_z, "gz")
-    total, first_y, first_z = pl.pallas_call(
+    total, turned = pl.pallas_call(
         functools.partial(local_kernel, slab_y, slab_z, count),
         out_shape=[
             jax.ShapeDtypeStruct((2 * width, 4 * width), jnp.float32),
-            jax.ShapeDtypeStruct((slab_z * rows, 2 * width), jnp.bfloat16),
-            jax.ShapeDtypeStruct((slab_y * rows, 2 * width), jnp.bfloat16),
+            jax.ShapeDtypeStruct((slab_y, slab_z, rows, width), jnp.bfloat16),
         ],
         scratch_shapes=[
             pltpu.VMEM((8 * sites * 24, 128), jnp.float32),
-            pltpu.VMEM((sites * rows, 2 * width), jnp.bfloat16),
             pltpu.VMEM((sites * rows, 6 * width), jnp.bfloat16),
         ],
         compiler_params=pltpu.CompilerParams(vmem_limit_bytes=32 * 1024 * 1024),
@@ -314,7 +317,7 @@
         out_shape=jax.ShapeDtypeStruct((8 * width, width), jnp.bfloat16),
         scratch_shapes=[pltpu.VMEM((8 * width, width), jnp.float32)],
         compiler_params=pltpu.CompilerParams(vmem_limit_bytes=16 * 1024 * 1024),
-    )(face_z, face_y, total, first_y, first_z)
+    )(face_z, face_y, total, inputs[0], turned)
     gathered = lax.all_to_all(partial.reshape(width, 8, width), ("gy", "gz"), 0, 0, tiled=True)
     mine = pl.pallas_call(
         sum_kernel,

time: 32.2 us -> 32.2 us (level)
  transfers between devices with their start and end apart: 2 -> 2, of which waited for: 1 -> 1; matrix products, arithmetic and copies ran while one was open for 0% -> 0% of each run, Pallas kernels for 12% -> 11%
where the time goes in v7:
time: 32.2 us; the launch traced here: 32.1 us
  blocking collectives  19.8 us (61%)
  Pallas kernels  6.4 us (20%)
  starting transfers between devices  4.25 us (13%)
  waiting for transfers between devices  1.64 us (5%)
    all_to_all x1, blocking collectives, per_device(): lax.all_to_all(partial.reshape(width, 8, width), ('gy', 'gz'), 0, 0, tile...  19.8 us
    ppermute x2, starting transfers between devices, shifted(): return lax.ppermute(block, axis, [(i, (i + 1) % size) for i in range(size)])  4.25 us
    pallas_call x1, Pallas kernels, per_device(): pl.pallas_call(functools.partial(local_kernel, slab_y, slab_z, count), ou...  3.58 us
    pallas_call x1, Pallas kernels, per_device(): pl.pallas_call(functools.partial(first_kernel, slab_y, slab_z, count), ou...  1.72 us
    ppermute x2, waiting for transfers between devices, shifted(): return lax.ppermute(block, axis, [(i, (i + 1) % size) for i in range(size)])  1.64 us
  transfers between devices with their start and end apart: 2, of which 1 were waited for; matrix products, arithmetic and copies ran while one was open for 0% of the time, Pallas kernels for 11%

profile of v7, /device:TPU:1, one launch (start us, length us, event | category | flops | bytes accessed | tf_op | source)
XLA Modules:
  0.0 32.1 jit_solution(6699045676748525758)
XLA Ops:
  0.0 1.7 %shard_map.55 = (bf16[384,128]{1,0:T(8,128)(2,1)S(1)}, bf16[768,128]{1,0:T(8,128)(2,1)S(1)}, bf16[8,4,96,128]{3,2,1,0:T(8,128)(2,1)S(1)}, f32[54,32,16]{2,1,0:T(...) custom-call(bf16[8,4,96,128]{3,2,1,0:T(8,128)(2,1)} %bitcast.12, ...), custom_call_target="tpu_custom_call" | custom-call | flops 2000000000 | bytes 600000 | tf_op jit(solution)/shard_map/pallas_call | solution.py:283
  1.7 2.2 %collective-permute-start.1 = (bf16[384,128]{1,0:T(8,128)(2,1)S(1)}, bf16[384,128]{1,0:T(8,128)(2,1)S(1)}, u32[]{:S(2)}, u32[]{:S(2)}) collective-permute-start(bf16[384,128]{1,0:T(8,128)(2,1)S(1)} %get-tuple-element.15), channel_id=1, source_target_pairs={{0,16},{16,32},{32,48},{48,64},{64,80},{80,96},{96,112},{112,0},{1... | collective-permute-start | bytes 294920 | tf_op jit(solution)/shard_map/ppermute | solution.py:271
  3.9 2.0 %collective-permute-start = (bf16[768,128]{1,0:T(8,128)(2,1)S(1)}, bf16[768,128]{1,0:T(8,128)(2,1)S(1)}, u32[]{:S(2)}, u32[]{:S(2)}) collective-permute-start(bf16[768,128]{1,0:T(8,128)(2,1)S(1)} %get-tuple-element.14), channel_id=1, source_target_pairs={{0,1},{1,2},{2,3},{3,4},{4,5},{5,6},{6,7},{7,8},{8,9},{9,10},{10,1... | collective-permute-start | bytes 589832 | tf_op jit(solution)/shard_map/ppermute | solution.py:271
  6.0 3.6 %shard_map.56 = (f32[256,512]{1,0:T(8,128)S(1)}, bf16[8,4,96,128]{3,2,1,0:T(8,128)(2,1)S(1)}) custom-call(bf16[8,4,96,128]{3,2,1,0:T(8,128)(2,1)S(1)} %get-tuple-element.16.v_ref, f32[54,32,16]{2,1,0:T(8,128)S(1)} %get-tuple-element.17.links, f32[2,96,128]{2,1,0:T(8,128)S(1)} %get-tuple-element.18.waves, bf16[2,128,256]{2,1,0:T(8,128)(2,1)S(1)} %get-tuple-element.19.spread, ...), custom_call_target="tpu_custom_call" | custom-call | flops 5000000000 | bytes 4000000 | tf_op jit(solution)/shard_map/pallas_call | solution.py:302
  9.6 1.6 %collective-permute-done.1.face_y = bf16[384,128]{1,0:T(8,128)(2,1)S(1)} collective-permute-done((bf16[384,128]{1,0:T(8,128)(2,1)S(1)}, bf16[384,128]{1,0:T(8,128)(2,1)S(1)}, u32[]{:S(2)}, u32[]{:S(2)}) %collective-permute-start.1) | collective-permute-done | bytes 98336 | tf_op jit(solution)/shard_map/ppermute | solution.py:271
  11.2 0.0 collective-permute-done.face_z
  11.2 0.5 %shard_map.57 = bf16[1024,128]{1,0:T(8,128)(2,1)S(1)} custom-call(bf16[768,128]{1,0:T(8,128)(2,1)S(1)} %collective-permute-done.face_z, bf16[384,128]{1,0:T(8,128)(2,1)S(1)} %collective-permute-done.1.face_y, f32[256,512]{1,0:T(8,128)S(1)} %get-tuple-element.21.total, bf16[8,4,96,128]{3,2,1,0:T(8,128)(2,1)S(1)} %get-tuple-element.16.v_ref, ...), custom_call_target="tpu_custom_call" | custom-call | tf_op jit(solution)/shard_map/pallas_call | solution.py:315
  11.7 19.8 %all_to_all.5 = bf16[128,8,128]{2,1,0:T(8,128)(2,1)S(1)} all-to-all(bf16[128,8,128]{2,1,0:T(8,128)(2,1)S(1)} %bitcast.10), channel_id=1, replica_groups=mesh['gy'=8,'gz'=16] {'gy','gz'}, dimensions={0} | all-to-all | bytes 524288 | tf_op jit(solution)/shard_map/all_to_all | solution.py:321
  31.5 0.6 %shard_map.58 = f32[8,128]{1,0:T(8,128)} custom-call(bf16[1024,128]{1,0:T(8,128)(2,1)S(1)} %bitcast.9), custom_call_target="tpu_custom_call" | custom-call | tf_op jit(solution)/shard_map/pallas_call | solution.py:322
Async XLA Ops:
  1.7 9.5 %collective-permute-start.1 = (bf16[384,128]{1,0:T(8,128)(2,1)S(1)}, bf16[384,128]{1,0:T(8,128)(2,1)S(1)}, u32[]{:S(2)}, u32[]{:S(2)}) collective-permute-start(bf16[384,128]{1,0:T(8,128)(2,1)S(1)} %get-tuple-element.15), channel_id=1, source_target_pairs={{0,16},{16,32},{32,48},{48,64},{64,80},{80,96},{96,112},{112,0},{1... | collective-permute-start | bytes 294920 | tf_op jit(solution)/shard_map/ppermute | solution.py:271
  3.9 7.3 %collective-permute-start = (bf16[768,128]{1,0:T(8,128)(2,1)S(1)}, bf16[768,128]{1,0:T(8,128)(2,1)S(1)}, u32[]{:S(2)}, u32[]{:S(2)}) collective-permute-start(bf16[768,128]{1,0:T(8,128)(2,1)S(1)} %get-tuple-element.14), channel_id=1, source_target_pairs={{0,1},{1,2},{2,3},{3,4},{4,5},{5,6},{6,7},{7,8},{8,9},{9,10},{10,1... | collective-permute-start | bytes 589832 | tf_op jit(solution)/shard_map/ppermute | solution.py:271

commit v8 on v7

--- a/solution.py
+++ b/solution.py
@@ -49,7 +49,9 @@
 def spread_links(flat, spread):
     high = flat.astype(jnp.bfloat16)
     low = (flat - high.astype(jnp.float32)).astype(jnp.bfloat16)
-    return [jnp.dot(half, spread, preferred_element_type=jnp.float32) for half in (high, low)]
+    both = jnp.concatenate([high, low], axis=0)
+    both = jnp.dot(both, spread, preferred_element_type=jnp.float32)
+    return both[: flat.shape[0]], both[flat.shape[0] :]
 
 
 def store_coefs(coefs, base, stride, wide, sites):
@@ -125,9 +127,10 @@
         move.wait()
     flat[...] = back_links(links, 2, 0, sites, count)
     edge = flat[pl.ds(slab_z - 1, 3 * slab_y, stride=slab_z), :]
-    store_coefs(coefs_z, 0, slab_y * 24, spread_links(edge, spread[0]), slab_y)
-    edge = back_links(links, 1, sites - 8, 8, count)
-    store_coefs(coefs_y, 0, 8 * 24, spread_links(edge, spread[0]), 8)
+    edge = jnp.concatenate([edge, back_links(links, 1, sites - 8, 8, count)], axis=0)
+    wide = spread_links(edge, spread[0])
+    store_coefs(coefs_z, 0, slab_y * 24, [half[: 3 * slab_y] for half in wide], slab_y)
+    store_coefs(coefs_y, 0, 8 * 24, [half[3 * slab_y :] for half in wide], 8)
     for move in moves[3:6]:
         move.wait()
     mask = masks[0]
@@ -144,12 +147,14 @@
 
 
 def local_kernel(
-    slab_y, slab_z, count, v_ref, links, waves, spread, masks, total, turned, coefs, right
+    slab_y, slab_z, count, v_ref, links, waves, spread, masks, total, first_y, first_z,
+    turned, coefs, right,
 ):
     rows = 6 * count
     sites = slab_y * slab_z
     width = v_ref.shape[-1]
 
+    tables = []
     for direction in range(3):
         flat = []
         for colour in range(3):
@@ -159,10 +164,14 @@
                     pieces.append(links[((direction * 2 + part) * 3 + colour) * 3 + other])
             pieces.append(jnp.zeros((sites, 128 - rows), jnp.float32))
             flat.append(jnp.concatenate(pieces, axis=1))
-        wide = spread_links(jnp.concatenate(flat, axis=0), spread[1 if direction == 0 else 0])
-        store_coefs(coefs, direction * sites * 24, 4 * sites * 24, wide, sites)
-    wide = spread_links(back_links(links, 0, 0, sites, count), spread[0])
-    store_coefs(coefs, 3 * sites * 24, 4 * sites * 24, wide, sites)
+        tables.append(jnp.concatenate(flat, axis=0))
+    tables.append(back_links(links, 0, 0, sites, count))
+    wide = spread_links(tables[0], spread[1])
+    store_coefs(coefs, 0, 4 * sites * 24, wide, sites)
+    wide = spread_links(jnp.concatenate(tables[1:], axis=0), spread[0])
+    for i in range(3):
+        mine = [half[3 * sites * i : 3 * sites * (i + 1)] for half in wide]
+        store_coefs(coefs, (i + 1) * sites * 24, 4 * sites * 24, mine, sites)
 
     mask = [masks[i] for i in range(3)]
 
@@ -219,6 +228,9 @@
     last = pl.ds((slab_y - 1) * slab_z * rows, slab_z * rows)
     right[last, 2 * width : 3 * width] = jnp.zeros((slab_z * rows, width), jnp.bfloat16)
     right[last, 4 * width : 5 * width] = jnp.zeros((slab_z * rows, width), jnp.bfloat16)
+    for first, of in ((first_y, (0,)), (first_z, (slice(None), 0))):
+        parts = [ref[of].reshape(-1, width) for ref in (v_ref, turned)]
+        first[...] = jnp.concatenate(parts, axis=1).T
     left = jnp.concatenate(
         [v_ref[...].reshape(sites * rows, width), turned[...].reshape(sites * rows, width)], axis=1
     )
@@ -229,19 +241,13 @@
     total[:, 2 * width :] = both[:, 2 * width : 4 * width] + both[:, 4 * width :]
 
 
-def edge_kernel(scale, face_z, face_y, total, v_ref, turned, out, sums):
+def edge_kernel(scale, face_z, face_y, total, first_y, first_z, out, sums):
     width = face_y.shape[1]
 
-    def product(parts, face):
-        first = jnp.concatenate([part.reshape(face.shape) for part in parts], axis=1)
-        return lax.dot_general(
-            first, face[...], (((0,), (0,)), ((), ())), preferred_element_type=jnp.float32
-        )
-
-    extra = {
-        2: product((v_ref[0], turned[0]), face_y),
-        3: product((v_ref[:, 0], turned[:, 0]), face_z),
-    }
+    def product(first, face):
+        return jnp.dot(first[...], face[...], preferred_element_type=jnp.float32)
+
+    extra = {2: product(first_y, face_y), 3: product(first_z, face_z)}
     for operator in range(4):
         both = total[:, operator * width : (operator + 1) * width]
         if operator in extra:
@@ -299,13 +305,15 @@
     )(*(pltpu.with_memory_space_constraint(each, pltpu.HBM) for each in inputs))
     face_y = shifted(face_y, "gy")
     face_z = shifted(face_z, "gz")
-    total, turned = pl.pallas_call(
+    total, first_y, first_z = pl.pallas_call(
         functools.partial(local_kernel, slab_y, slab_z, count),
         out_shape=[
             jax.ShapeDtypeStruct((2 * width, 4 * width), jnp.float32),
-            jax.ShapeDtypeStruct((slab_y, slab_z, rows, width), jnp.bfloat16),
+            jax.ShapeDtypeStruct((2 * width, slab_z * rows), jnp.bfloat16),
+            jax.ShapeDtypeStruct((2 * width, slab_y * rows), jnp.bfloat16),
         ],
         scratch_shapes=[
+            pltpu.VMEM((slab_y, slab_z, rows, width), jnp.bfloat16),
             pltpu.VMEM((8 * sites * 24, 128), jnp.float32),
             pltpu.VMEM((sites * rows, 6 * width), jnp.bfloat16),
         ],
@@ -317,7 +325,7 @@
         out_shape=jax.ShapeDtypeStruct((8 * width, width), jnp.bfloat16),
         scratch_shapes=[pltpu.VMEM((8 * width, width), jnp.float32)],
         compiler_params=pltpu.CompilerParams(vmem_limit_bytes=16 * 1024 * 1024),
-    )(face_z, face_y, total, inputs[0], turned)
+    )(face_z, face_y, total, first_y, first_z)
     gathered = lax.all_to_all(partial.reshape(width, 8, width), ("gy", "gz"), 0, 0, tiled=True)
     mine = pl.pallas_call(
         sum_kernel,

time: 32.2 us -> 32.2 us (level)
  no operation moved by 1% of the time
where the time goes in v8:
time: 32.2 us; the launch traced here: 32.1 us
  blocking collectives  19.8 us (61%)
  Pallas kernels  6.32 us (20%)
  starting transfers between devices  4.24 us (13%)
  waiting for transfers between devices  1.7 us (5%)
    all_to_all x1, blocking collectives, per_device(): lax.all_to_all(partial.reshape(width, 8, width), ('gy', 'gz'), 0, 0, tile...  19.8 us
    ppermute x2, starting transfers between devices, shifted(): return lax.ppermute(block, axis, [(i, (i + 1) % size) for i in range(size)])  4.24 us
    pallas_call x1, Pallas kernels, per_device(): pl.pallas_call(functools.partial(local_kernel, slab_y, slab_z, count), ou...  3.52 us
    pallas_call x1, Pallas kernels, per_device(): pl.pallas_call(functools.partial(first_kernel, slab_y, slab_z, count), ou...  1.75 us
    ppermute x2, waiting for transfers between devices, shifted(): return lax.ppermute(block, axis, [(i, (i + 1) % size) for i in range(size)])  1.7 us
  transfers between devices with their start and end apart: 2, of which 1 were waited for; matrix products, arithmetic and copies ran while one was open for 0% of the time, Pallas kernels for 11%

profile of v8, /device:TPU:1, one launch (start us, length us, event | category | flops | bytes accessed | tf_op | source)
XLA Modules:
  0.0 32.1 jit_solution(6739040026140242011)
XLA Ops:
  0.0 1.8 %shard_map.55 = (bf16[384,128]{1,0:T(8,128)(2,1)S(1)}, bf16[768,128]{1,0:T(8,128)(2,1)S(1)}, bf16[8,4,96,128]{3,2,1,0:T(8,128)(2,1)S(1)}, f32[54,32,16]{2,1,0:T(...) custom-call(bf16[8,4,96,128]{3,2,1,0:T(8,128)(2,1)} %bitcast.12, ...), custom_call_target="tpu_custom_call" | custom-call | flops 2000000000 | bytes 600000 | tf_op jit(solution)/shard_map/pallas_call | solution.py:289
  1.8 2.2 %collective-permute-start.1 = (bf16[384,128]{1,0:T(8,128)(2,1)S(1)}, bf16[384,128]{1,0:T(8,128)(2,1)S(1)}, u32[]{:S(2)}, u32[]{:S(2)}) collective-permute-start(bf16[384,128]{1,0:T(8,128)(2,1)S(1)} %get-tuple-element.16), channel_id=1, source_target_pairs={{0,16},{16,32},{32,48},{48,64},{64,80},{80,96},{96,112},{112,0},{1... | collective-permute-start | bytes 294920 | tf_op jit(solution)/shard_map/ppermute | solution.py:277
  4.0 2.1 %collective-permute-start = (bf16[768,128]{1,0:T(8,128)(2,1)S(1)}, bf16[768,128]{1,0:T(8,128)(2,1)S(1)}, u32[]{:S(2)}, u32[]{:S(2)}) collective-permute-start(bf16[768,128]{1,0:T(8,128)(2,1)S(1)} %get-tuple-element.15), channel_id=1, source_target_pairs={{0,1},{1,2},{2,3},{3,4},{4,5},{5,6},{6,7},{7,8},{8,9},{9,10},{10,1... | collective-permute-start | bytes 589832 | tf_op jit(solution)/shard_map/ppermute | solution.py:277
  6.0 3.5 %shard_map.56 = (f32[256,512]{1,0:T(8,128)S(1)}, bf16[256,384]{1,0:T(8,128)(2,1)S(1)}, bf16[256,768]{1,0:T(8,128)(2,1)S(1)}) custom-call(bf16[8,4,96,128]{3,2,1,0:T(8,128)(2,1)S(1)} %get-tuple-element.17.v_ref, f32[54,32,16]{2,1,0:T(8,128)S(1)} %get-tuple-element.18.links, f32[2,96,128]{2,1,0:T(8,128)S(1)} %get-tuple-element.19.waves, ...), custom_call_target="tpu_custom_call" | custom-call | flops 5000000000 | bytes 4000000 | tf_op jit(solution)/shard_map/pallas_call | solution.py:308
  9.5 1.7 %collective-permute-done.1.face_y = bf16[384,128]{1,0:T(8,128)(2,1)S(1)} collective-permute-done((bf16[384,128]{1,0:T(8,128)(2,1)S(1)}, bf16[384,128]{1,0:T(8,128)(2,1)S(1)}, u32[]{:S(2)}, u32[]{:S(2)}) %collective-permute-start.1) | collective-permute-done | bytes 98336 | tf_op jit(solution)/shard_map/ppermute | solution.py:277
  11.2 0.0 collective-permute-done.face_z
  11.2 0.4 %shard_map.57 = bf16[1024,128]{1,0:T(8,128)(2,1)S(1)} custom-call(bf16[768,128]{1,0:T(8,128)(2,1)S(1)} %collective-permute-done.face_z, bf16[384,128]{1,0:T(8,128)(2,1)S(1)} %collective-permute-done.1.face_y, f32[256,512]{1,0:T(8,128)S(1)} %get-tuple-element.22.total, bf16[256,384]{1,0:T(8,128)(2,1)S(1)} %get-tuple-element.23.first_y, ...), custom_call_target="tpu_custom_call" | custom-call | tf_op jit(solution)/shard_map/pallas_call | solution.py:323
  11.7 19.8 %all_to_all.5 = bf16[128,8,128]{2,1,0:T(8,128)(2,1)S(1)} all-to-all(bf16[128,8,128]{2,1,0:T(8,128)(2,1)S(1)} %bitcast.9), channel_id=1, replica_groups=mesh['gy'=8,'gz'=16] {'gy','gz'}, dimensions={0} | all-to-all | bytes 524288 | tf_op jit(solution)/shard_map/all_to_all | solution.py:329
  31.4 0.6 %shard_map.58 = f32[8,128]{1,0:T(8,128)} custom-call(bf16[1024,128]{1,0:T(8,128)(2,1)S(1)} %bitcast.10), custom_call_target="tpu_custom_call" | custom-call | tf_op jit(solution)/shard_map/pallas_call | solution.py:330
Async XLA Ops:
  1.8 9.5 %collective-permute-start.1 = (bf16[384,128]{1,0:T(8,128)(2,1)S(1)}, bf16[384,128]{1,0:T(8,128)(2,1)S(1)}, u32[]{:S(2)}, u32[]{:S(2)}) collective-permute-start(bf16[384,128]{1,0:T(8,128)(2,1)S(1)} %get-tuple-element.16), channel_id=1, source_target_pairs={{0,16},{16,32},{32,48},{48,64},{64,80},{80,96},{96,112},{112,0},{1... | collective-permute-start | bytes 294920 | tf_op jit(solution)/shard_map/ppermute | solution.py:277
  4.0 7.3 %collective-permute-start = (bf16[768,128]{1,0:T(8,128)(2,1)S(1)}, bf16[768,128]{1,0:T(8,128)(2,1)S(1)}, u32[]{:S(2)}, u32[]{:S(2)}) collective-permute-start(bf16[768,128]{1,0:T(8,128)(2,1)S(1)} %get-tuple-element.15), channel_id=1, source_target_pairs={{0,1},{1,2},{2,3},{3,4},{4,5},{5,6},{6,7},{7,8},{8,9},{9,10},{10,1... | collective-permute-start | bytes 589832 | tf_op jit(solution)/shard_map/ppermute | solution.py:277

commit v9 on v8

--- a/solution.py
+++ b/solution.py
@@ -120,8 +120,8 @@
         pltpu.make_async_copy(source.at[where], target.at[where], sems.at[i])
         for i, (source, target, where) in enumerate(pairs)
     ]
-    for move in moves:
-        move.start()
+    for i, move in enumerate(moves):
+        move.start(priority=0 if i < 6 else 1)
     rows = 6 * count
     for move in moves[:3]:
         move.wait()

time: 32.2 us -> 32.2 us (level)
  no operation moved by 1% of the time
where the time goes in v9:
time: 32.2 us; the launch traced here: 32.1 us
  blocking collectives  19.8 us (61%)
  Pallas kernels  6.32 us (20%)
  starting transfers between devices  4.24 us (13%)
  waiting for transfers between devices  1.7 us (5%)
    all_to_all x1, blocking collectives, per_device(): lax.all_to_all(partial.reshape(width, 8, width), ('gy', 'gz'), 0, 0, tile...  19.8 us
    ppermute x2, starting transfers between devices, shifted(): return lax.ppermute(block, axis, [(i, (i + 1) % size) for i in range(size)])  4.24 us
    pallas_call x1, Pallas kernels, per_device(): pl.pallas_call(functools.partial(local_kernel, slab_y, slab_z, count), ou...  3.52 us
    pallas_call x1, Pallas kernels, per_device(): pl.pallas_call(functools.partial(first_kernel, slab_y, slab_z, count), ou...  1.75 us
    ppermute x2, waiting for transfers between devices, shifted(): return lax.ppermute(block, axis, [(i, (i + 1) % size) for i in range(size)])  1.7 us
  transfers between devices with their start and end apart: 2, of which 1 were waited for; matrix products, arithmetic and copies ran while one was open for 0% of the time, Pallas kernels for 11%

profile of v9, /device:TPU:1, one launch (start us, length us, event | category | flops | bytes accessed | tf_op | source)
XLA Modules:
  0.0 32.1 jit_solution(14553291012946892114)
XLA Ops:
  0.0 1.8 %shard_map.55 = (bf16[384,128]{1,0:T(8,128)(2,1)S(1)}, bf16[768,128]{1,0:T(8,128)(2,1)S(1)}, bf16[8,4,96,128]{3,2,1,0:T(8,128)(2,1)S(1)}, f32[54,32,16]{2,1,0:T(...) custom-call(bf16[8,4,96,128]{3,2,1,0:T(8,128)(2,1)} %bitcast.12, ...), custom_call_target="tpu_custom_call" | custom-call | flops 2000000000 | bytes 600000 | tf_op jit(solution)/shard_map/pallas_call | solution.py:289
  1.8 2.2 %collective-permute-start.1 = (bf16[384,128]{1,0:T(8,128)(2,1)S(1)}, bf16[384,128]{1,0:T(8,128)(2,1)S(1)}, u32[]{:S(2)}, u32[]{:S(2)}) collective-permute-start(bf16[384,128]{1,0:T(8,128)(2,1)S(1)} %get-tuple-element.16), channel_id=1, source_target_pairs={{0,16},{16,32},{32,48},{48,64},{64,80},{80,96},{96,112},{112,0},{1... | collective-permute-start | bytes 294920 | tf_op jit(solution)/shard_map/ppermute | solution.py:277
  4.0 2.1 %collective-permute-start = (bf16[768,128]{1,0:T(8,128)(2,1)S(1)}, bf16[768,128]{1,0:T(8,128)(2,1)S(1)}, u32[]{:S(2)}, u32[]{:S(2)}) collective-permute-start(bf16[768,128]{1,0:T(8,128)(2,1)S(1)} %get-tuple-element.15), channel_id=1, source_target_pairs={{0,1},{1,2},{2,3},{3,4},{4,5},{5,6},{6,7},{7,8},{8,9},{9,10},{10,1... | collective-permute-start | bytes 589832 | tf_op jit(solution)/shard_map/ppermute | solution.py:277
  6.0 3.5 %shard_map.56 = (f32[256,512]{1,0:T(8,128)S(1)}, bf16[256,384]{1,0:T(8,128)(2,1)S(1)}, bf16[256,768]{1,0:T(8,128)(2,1)S(1)}) custom-call(bf16[8,4,96,128]{3,2,1,0:T(8,128)(2,1)S(1)} %get-tuple-element.17.v_ref, f32[54,32,16]{2,1,0:T(8,128)S(1)} %get-tuple-element.18.links, f32[2,96,128]{2,1,0:T(8,128)S(1)} %get-tuple-element.19.waves, ...), custom_call_target="tpu_custom_call" | custom-call | flops 5000000000 | bytes 4000000 | tf_op jit(solution)/shard_map/pallas_call | solution.py:308
  9.5 1.7 %collective-permute-done.1.face_y = bf16[384,128]{1,0:T(8,128)(2,1)S(1)} collective-permute-done((bf16[384,128]{1,0:T(8,128)(2,1)S(1)}, bf16[384,128]{1,0:T(8,128)(2,1)S(1)}, u32[]{:S(2)}, u32[]{:S(2)}) %collective-permute-start.1) | collective-permute-done | bytes 98336 | tf_op jit(solution)/shard_map/ppermute | solution.py:277
  11.2 0.0 collective-permute-done.face_z
  11.2 0.4 %shard_map.57 = bf16[1024,128]{1,0:T(8,128)(2,1)S(1)} custom-call(bf16[768,128]{1,0:T(8,128)(2,1)S(1)} %collective-permute-done.face_z, bf16[384,128]{1,0:T(8,128)(2,1)S(1)} %collective-permute-done.1.face_y, f32[256,512]{1,0:T(8,128)S(1)} %get-tuple-element.22.total, bf16[256,384]{1,0:T(8,128)(2,1)S(1)} %get-tuple-element.23.first_y, ...), custom_call_target="tpu_custom_call" | custom-call | tf_op jit(solution)/shard_map/pallas_call | solution.py:323
  11.7 19.8 %all_to_all.5 = bf16[128,8,128]{2,1,0:T(8,128)(2,1)S(1)} all-to-all(bf16[128,8,128]{2,1,0:T(8,128)(2,1)S(1)} %bitcast.9), channel_id=1, replica_groups=mesh['gy'=8,'gz'=16] {'gy','gz'}, dimensions={0} | all-to-all | bytes 524288 | tf_op jit(solution)/shard_map/all_to_all | solution.py:329
  31.4 0.6 %shard_map.58 = f32[8,128]{1,0:T(8,128)} custom-call(bf16[1024,128]{1,0:T(8,128)(2,1)S(1)} %bitcast.10), custom_call_target="tpu_custom_call" | custom-call | tf_op jit(solution)/shard_map/pallas_call | solution.py:330
Async XLA Ops:
  1.8 9.5 %collective-permute-start.1 = (bf16[384,128]{1,0:T(8,128)(2,1)S(1)}, bf16[384,128]{1,0:T(8,128)(2,1)S(1)}, u32[]{:S(2)}, u32[]{:S(2)}) collective-permute-start(bf16[384,128]{1,0:T(8,128)(2,1)S(1)} %get-tuple-element.16), channel_id=1, source_target_pairs={{0,16},{16,32},{32,48},{48,64},{64,80},{80,96},{96,112},{112,0},{1... | collective-permute-start | bytes 294920 | tf_op jit(solution)/shard_map/ppermute | solution.py:277
  4.0 7.3 %collective-permute-start = (bf16[768,128]{1,0:T(8,128)(2,1)S(1)}, bf16[768,128]{1,0:T(8,128)(2,1)S(1)}, u32[]{:S(2)}, u32[]{:S(2)}) collective-permute-start(bf16[768,128]{1,0:T(8,128)(2,1)S(1)} %get-tuple-element.15), channel_id=1, source_target_pairs={{0,1},{1,2},{2,3},{3,4},{4,5},{5,6},{6,7},{7,8},{8,9},{9,10},{10,1... | collective-permute-start | bytes 589832 | tf_op jit(solution)/shard_map/ppermute | solution.py:277

commit v10 on v8

--- a/solution.py
+++ b/solution.py
@@ -318,7 +318,7 @@
             pltpu.VMEM((sites * rows, 6 * width), jnp.bfloat16),
         ],
         compiler_params=pltpu.CompilerParams(vmem_limit_bytes=32 * 1024 * 1024),
-        cost_estimate=pl.CostEstimate(flops=5_000_000_000, bytes_accessed=4_000_000, transcendentals=0),
+        cost_estimate=pl.CostEstimate(flops=500_000_000, bytes_accessed=1_000_000, transcendentals=0),
     )(*inputs)
     partial = pl.pallas_call(
         functools.partial(edge_kernel, scale),

time: 32.2 us -> 32.3 us (level)
  waiting for transfers between devices: 1.7 us -> 4.94 us
  blocking collectives: 19.8 us -> 16.9 us
    ppermute x2, waiting for transfers between devices: 1.7 us -> 4.94 us  [shifted(): return lax.ppermute(block, axis, [(i, (i + 1) % size) for i in range(size)])]
    all_to_all x1, blocking collectives: 19.8 us -> 16.9 us  [per_device(): lax.all_to_all(partial.reshape(width, 8, width), ('gy', 'gz'), 0, 0, tile...]
where the time goes in v10:
time: 32.3 us; the launch traced here: 32.2 us
  blocking collectives  16.9 us (52%)
  Pallas kernels  6.33 us (20%)
  waiting for transfers between devices  4.94 us (15%)
  starting transfers between devices  3.96 us (12%)
    all_to_all x1, blocking collectives, per_device(): lax.all_to_all(partial.reshape(width, 8, width), ('gy', 'gz'), 0, 0, tile...  16.9 us
    ppermute x2, waiting for transfers between devices, shifted(): return lax.ppermute(block, axis, [(i, (i + 1) % size) for i in range(size)])  4.94 us
    ppermute x2, starting transfers between devices, shifted(): return lax.ppermute(block, axis, [(i, (i + 1) % size) for i in range(size)])  3.96 us
    pallas_call x1, Pallas kernels, per_device(): pl.pallas_call(functools.partial(local_kernel, slab_y, slab_z, count), ou...  3.52 us
    pallas_call x1, Pallas kernels, per_device(): pl.pallas_call(functools.partial(first_kernel, slab_y, slab_z, count), ou...  1.75 us
  transfers between devices with their start and end apart: 2, of which 1 were waited for; matrix products, arithmetic and copies ran while one was open for 0% of the time, Pallas kernels for 11%

profile of v10, /device:TPU:1, one launch (start us, length us, event | category | flops | bytes accessed | tf_op | source)
XLA Modules:
  0.0 32.2 jit_solution(3045518545352358428)
XLA Ops:
  0.0 1.8 %shard_map.55 = (bf16[384,128]{1,0:T(8,128)(2,1)S(1)}, bf16[768,128]{1,0:T(8,128)(2,1)S(1)}, bf16[8,4,96,128]{3,2,1,0:T(8,128)(2,1)S(1)}, f32[54,32,16]{2,1,0:T(...) custom-call(bf16[8,4,96,128]{3,2,1,0:T(8,128)(2,1)} %bitcast.12, ...), custom_call_target="tpu_custom_call" | custom-call | flops 2000000000 | bytes 600000 | tf_op jit(solution)/shard_map/pallas_call | solution.py:289
  1.8 2.7 %collective-permute-start = (bf16[768,128]{1,0:T(8,128)(2,1)S(1)}, bf16[768,128]{1,0:T(8,128)(2,1)S(1)}, u32[]{:S(2)}, u32[]{:S(2)}) collective-permute-start(bf16[768,128]{1,0:T(8,128)(2,1)S(1)} %get-tuple-element.15), channel_id=1, source_target_pairs={{0,1},{1,2},{2,3},{3,4},{4,5},{5,6},{6,7},{7,8},{8,9},{9,10},{10,1... | collective-permute-start | bytes 589832 | tf_op jit(solution)/shard_map/ppermute | solution.py:277
  4.4 1.3 %collective-permute-start.1 = (bf16[384,128]{1,0:T(8,128)(2,1)S(1)}, bf16[384,128]{1,0:T(8,128)(2,1)S(1)}, u32[]{:S(2)}, u32[]{:S(2)}) collective-permute-start(bf16[384,128]{1,0:T(8,128)(2,1)S(1)} %get-tuple-element.16), channel_id=1, source_target_pairs={{0,16},{16,32},{32,48},{48,64},{64,80},{80,96},{96,112},{112,0},{1... | collective-permute-start | bytes 294920 | tf_op jit(solution)/shard_map/ppermute | solution.py:277
  5.7 3.5 %shard_map.56 = (f32[256,512]{1,0:T(8,128)S(1)}, bf16[256,384]{1,0:T(8,128)(2,1)S(1)}, bf16[256,768]{1,0:T(8,128)(2,1)S(1)}) custom-call(bf16[8,4,96,128]{3,2,1,0:T(8,128)(2,1)S(1)} %get-tuple-element.17.v_ref, f32[54,32,16]{2,1,0:T(8,128)S(1)} %get-tuple-element.18.links, f32[2,96,128]{2,1,0:T(8,128)S(1)} %get-tuple-element.19.waves, ...), custom_call_target="tpu_custom_call" | custom-call | flops 500000000 | bytes 1000000 | tf_op jit(solution)/shard_map/pallas_call | solution.py:308
  9.3 4.9 %collective-permute-done.1.face_y = bf16[384,128]{1,0:T(8,128)(2,1)S(1)} collective-permute-done((bf16[384,128]{1,0:T(8,128)(2,1)S(1)}, bf16[384,128]{1,0:T(8,128)(2,1)S(1)}, u32[]{:S(2)}, u32[]{:S(2)}) %collective-permute-start.1) | collective-permute-done | bytes 98336 | tf_op jit(solution)/shard_map/ppermute | solution.py:277
  14.2 0.0 collective-permute-done.face_z
  14.2 0.4 %shard_map.57 = bf16[1024,128]{1,0:T(8,128)(2,1)S(1)} custom-call(bf16[768,128]{1,0:T(8,128)(2,1)S(1)} %collective-permute-done.face_z, bf16[384,128]{1,0:T(8,128)(2,1)S(1)} %collective-permute-done.1.face_y, f32[256,512]{1,0:T(8,128)S(1)} %get-tuple-element.22.total, bf16[256,384]{1,0:T(8,128)(2,1)S(1)} %get-tuple-element.23.first_y, ...), custom_call_target="tpu_custom_call" | custom-call | tf_op jit(solution)/shard_map/pallas_call | solution.py:323
  14.6 16.9 %all_to_all.5 = bf16[128,8,128]{2,1,0:T(8,128)(2,1)S(1)} all-to-all(bf16[128,8,128]{2,1,0:T(8,128)(2,1)S(1)} %bitcast.9), channel_id=1, replica_groups=mesh['gy'=8,'gz'=16] {'gy','gz'}, dimensions={0} | all-to-all | bytes 524288 | tf_op jit(solution)/shard_map/all_to_all | solution.py:329
  31.5 0.6 %shard_map.58 = f32[8,128]{1,0:T(8,128)} custom-call(bf16[1024,128]{1,0:T(8,128)(2,1)S(1)} %bitcast.10), custom_call_target="tpu_custom_call" | custom-call | tf_op jit(solution)/shard_map/pallas_call | solution.py:330
Async XLA Ops:
  1.8 12.4 %collective-permute-start = (bf16[768,128]{1,0:T(8,128)(2,1)S(1)}, bf16[768,128]{1,0:T(8,128)(2,1)S(1)}, u32[]{:S(2)}, u32[]{:S(2)}) collective-permute-start(bf16[768,128]{1,0:T(8,128)(2,1)S(1)} %get-tuple-element.15), channel_id=1, source_target_pairs={{0,1},{1,2},{2,3},{3,4},{4,5},{5,6},{6,7},{7,8},{8,9},{9,10},{10,1... | collective-permute-start | bytes 589832 | tf_op jit(solution)/shard_map/ppermute | solution.py:277
  4.4 9.8 %collective-permute-start.1 = (bf16[384,128]{1,0:T(8,128)(2,1)S(1)}, bf16[384,128]{1,0:T(8,128)(2,1)S(1)}, u32[]{:S(2)}, u32[]{:S(2)}) collective-permute-start(bf16[384,128]{1,0:T(8,128)(2,1)S(1)} %get-tuple-element.16), channel_id=1, source_target_pairs={{0,16},{16,32},{32,48},{48,64},{64,80},{80,96},{96,112},{112,0},{1... | collective-permute-start | bytes 294920 | tf_op jit(solution)/shard_map/ppermute | solution.py:277
